TPU v7x, 32 devices: a whole 2x2x4 slice. The times are simulated.
32 devices in a mesh: seq: 16 (over z, x, core), fsdp: 2 (over y).
Axes of the slice: x: 2, y: 2, z: 4, core: 2. Of those that a mesh axis runs over, the one named last changes fastest.
Arguments:
- tokens: bfloat16 [2, 2048, 640], P('fsdp', 'seq'), may hold values from -30 to 30, as said below
- w_q: bfloat16 [640, 1024], P(None, 'fsdp'), may hold values from -0.25 to 0.25
- w_k: bfloat16 [640, 256], P(None, 'fsdp'), may hold values from -0.25 to 0.25
- w_v: bfloat16 [640, 256], P(None, 'fsdp'), may hold values from -0.25 to 0.25
- w_o: bfloat16 [1024, 640], P('fsdp'), may hold values from -0.1875 to 0.1875
- w_gate: bfloat16 [640, 2048], P(None, 'fsdp'), may hold values from -0.25 to 0.25
- w_up: bfloat16 [640, 2048], P(None, 'fsdp'), may hold values from -0.25 to 0.25
- w_down: bfloat16 [2048, 640], P('fsdp'), may hold values from -0.125 to 0.125
- gains: float32 [3072], replicated, may hold values from 0.25 to 1.75
- positions: int32 [2, 2048], P('fsdp', 'seq'), may hold values from 0 to 2173, as said below
- cotangent: bfloat16 [2, 2048, 640], P('fsdp', 'seq'), may hold values from -6 to 6
Outputs:
- outputs: bfloat16 [2, 2048, 640], P('fsdp', 'seq')
- d_tokens: float32 [2, 2048, 640], P('fsdp', 'seq')
- d_w_q: float32 [655360], P(('seq', 'fsdp'))
- d_w_k: float32 [163840], P(('seq', 'fsdp'))
- d_w_v: float32 [163840], P(('seq', 'fsdp'))
- d_w_o: float32 [655360], P(('seq', 'fsdp'))
- d_w_gate: float32 [1310720], P(('seq', 'fsdp'))
- d_w_up: float32 [1310720], P(('seq', 'fsdp'))
- d_w_down: float32 [1310720], P(('seq', 'fsdp'))
- d_gains: float32 [3072], P(('seq', 'fsdp'))
Inputs may be any that keep to these rules, and one draw needn't show every extreme that they name: `tokens`: activations of order one with row scales that differ. Each sequence holds three documents end to end, positions counting from 0 at a document's start: the first continues an earlier text from a drawn offset and ends within the first 128 tokens, the second ends within the last 128 tokens, the third runs to the sequence's end.
All inputs are finite; a program needn't handle non-finite values.
Results may differ from a plain program's by a relative error of at most 0.017.
Values may be sent and summed in bfloat16 or wider, within the bound.
A program may use at most 128 MiB of HBM per device.

v0:
```python
import jax
import jax.numpy as jnp
from jax import lax
from jax.sharding import PartitionSpec as P

D = 640
HEADS = 4
HD = 256
WINDOW = 512
TOK_DEV = 128


EPSILON = 1e-06
NEGATIVE = -1e30


def shifted(value, axis, steps):
    count = lax.axis_size(axis)
    leading, last = (max(0, -steps), min(count, count - steps))
    return lax.ppermute(value, axis, [(source, source + steps) for source in range(leading, last)])


def rms_norm(vector, gain_vec):
    return (
        vector * lax.rsqrt(jnp.mean(vector * vector, axis=-1, keepdims=True) + EPSILON) * gain_vec
    )


def rotate(vector, places):
    half_size = vector.shape[-1] // 2
    inverse = 10000.0 ** (-2.0 * jnp.arange(half_size, dtype=jnp.float32) / vector.shape[-1])
    angles = places.astype(jnp.float32)[:, None] * inverse[None, :]
    cosine = jnp.cos(angles)
    sine_part = jnp.sin(angles)
    if vector.ndim == 3:
        cosine = cosine[:, None, :]
        sine_part = sine_part[:, None, :]
    first_half = vector[..., :half_size]
    second = vector[..., half_size:]
    return jnp.concatenate(
        [first_half * cosine - second * sine_part, second * cosine + first_half * sine_part],
        axis=-1,
    )


def queries_keys(q_raw, k_raw, gain_query, gain_key, places):
    queries = rotate(rms_norm(q_raw.reshape(q_raw.shape[0], HEADS, HD), gain_query), places)
    return (queries, rotate(rms_norm(k_raw, gain_key), places))


def gelu_mix(gate_raw, up_raw):
    return jax.nn.gelu(gate_raw, approximate=True) * up_raw


def matmul(left_side, right_side):
    return jnp.dot(left_side, right_side, preferred_element_type=jnp.float32)


def inner_left(left_side, right_side):
    return lax.dot_general(
        left_side, right_side, (((0,), (0,)), ((), ())), preferred_element_type=jnp.float32
    )


def inner_right(left_side, right_side):
    return lax.dot_general(
        left_side, right_side, (((1,), (1,)), ((), ())), preferred_element_type=jnp.float32
    )


def per_device(tokens, w_q, w_k, w_v, w_o, w_gate, w_up, w_down, gains, positions, cotangent):
    tokens_f = tokens[0].astype(jnp.float32)
    places = positions[0]
    gathered = (
        lax.all_gather(w_q, "fsdp", axis=1, tiled=True),
        lax.all_gather(w_k, "fsdp", axis=1, tiled=True),
        lax.all_gather(w_v, "fsdp", axis=1, tiled=True),
        lax.all_gather(w_o, "fsdp", axis=0, tiled=True),
        lax.all_gather(w_gate, "fsdp", axis=1, tiled=True),
        lax.all_gather(w_up, "fsdp", axis=1, tiled=True),
        lax.all_gather(w_down, "fsdp", axis=0, tiled=True),
    )
    full_q, full_k, full_v, full_o, full_gate, full_up, full_down = gathered
    gain_in = gains[0:D]
    gain_attn = gains[D : 2 * D]
    gain_mlp = gains[2 * D : 3 * D]
    gain_out = gains[3 * D : 4 * D]
    gain_query = gains[4 * D : 4 * D + HD]
    gain_key = gains[4 * D + HD : 4 * D + 2 * HD]
    normed, pull_in = jax.vjp(rms_norm, tokens_f, gain_in)
    normed_b = normed.astype(jnp.bfloat16)
    q_raw = matmul(normed_b, full_q)
    k_raw = matmul(normed_b, full_k)
    v_raw = matmul(normed_b, full_v)

    def rotary(q_part, k_part, gq_part, gk_part):
        return queries_keys(q_part, k_part, gq_part, gk_part, places)

    (queries, keys_own), pull_rot = jax.vjp(rotary, q_raw, k_raw, gain_query, gain_key)
    queries_b = queries.astype(jnp.bfloat16)
    keys_b = keys_own.astype(jnp.bfloat16)
    values_b = v_raw.astype(jnp.bfloat16)
    reach = WINDOW // TOK_DEV
    key_list = []
    value_list = []
    for distance in range(reach, 0, -1):
        far_keys, far_values = shifted((keys_b, values_b), "seq", distance)
        key_list.append(far_keys)
        value_list.append(far_values)
    keys_all = jnp.concatenate(key_list + [keys_b], axis=0)
    values_all = jnp.concatenate(value_list + [values_b], axis=0)
    span = (reach + 1) * TOK_DEV
    row_ids = jnp.arange(TOK_DEV, dtype=jnp.int32)[:, None]
    col_ids = jnp.arange(span, dtype=jnp.int32)[None, :]
    offsets = row_ids - col_ids + reach * TOK_DEV
    first_key = (lax.axis_index("seq") - reach) * TOK_DEV
    allowed = (
        (offsets >= 0)
        & (offsets <= jnp.minimum(places[:, None], WINDOW - 1))
        & (first_key + col_ids >= 0)
    )
    factor = HD ** (-0.5)
    raw_scores = (
        jnp.einsum("thd,kd->htk", queries_b, keys_all, preferred_element_type=jnp.float32) * factor
    )
    scores = jnp.where(allowed[None], raw_scores, NEGATIVE)
    exponent = jnp.exp(scores - jnp.max(scores, axis=-1, keepdims=True))
    probs_f = exponent / jnp.sum(exponent, axis=-1, keepdims=True)
    probs_b = probs_f.astype(jnp.bfloat16)
    attended = jnp.einsum("htk,kd->thd", probs_b, values_all, preferred_element_type=jnp.float32)
    attended_b = attended.reshape(TOK_DEV, HEADS * HD).astype(jnp.bfloat16)
    attn_raw = matmul(attended_b, full_o)
    attn_normed, pull_attn = jax.vjp(rms_norm, attn_raw, gain_attn)
    residual = tokens_f + attn_normed
    ffn_in, pull_mlp = jax.vjp(rms_norm, residual, gain_mlp)
    ffn_b = ffn_in.astype(jnp.bfloat16)
    gate_raw = matmul(ffn_b, full_gate)
    up_raw = matmul(ffn_b, full_up)
    hidden, pull_mix = jax.vjp(gelu_mix, gate_raw, up_raw)
    hidden_b = hidden.astype(jnp.bfloat16)
    down_raw = matmul(hidden_b, full_down)
    down_normed, pull_out = jax.vjp(rms_norm, down_raw, gain_out)
    output_b = (residual + down_normed).astype(jnp.bfloat16)
    again = (
        lax.all_gather(w_q, "fsdp", axis=1, tiled=True),
        lax.all_gather(w_k, "fsdp", axis=1, tiled=True),
        lax.all_gather(w_v, "fsdp", axis=1, tiled=True),
        lax.all_gather(w_o, "fsdp", axis=0, tiled=True),
        lax.all_gather(w_gate, "fsdp", axis=1, tiled=True),
        lax.all_gather(w_up, "fsdp", axis=1, tiled=True),
        lax.all_gather(w_down, "fsdp", axis=0, tiled=True),
    )
    full_q, full_k, full_v, full_o, full_gate, full_up, full_down = again
    d_out = cotangent[0].astype(jnp.float32)
    d_down, d_gain_out = pull_out(d_out)
    d_down_b = d_down.astype(jnp.bfloat16)
    grad_down = inner_left(hidden_b, d_down_b)
    d_hidden = inner_right(d_down_b, full_down)
    d_gate, d_up = pull_mix(d_hidden)
    d_gate_b = d_gate.astype(jnp.bfloat16)
    d_up_b = d_up.astype(jnp.bfloat16)
    grad_gate = inner_left(ffn_b, d_gate_b)
    grad_up = inner_left(ffn_b, d_up_b)
    d_ffn = inner_right(d_gate_b, full_gate) + inner_right(d_up_b, full_up)
    d_from_mlp, d_gain_mlp = pull_mlp(d_ffn)
    d_residual = d_out + d_from_mlp
    d_attn, d_gain_attn = pull_attn(d_residual)
    d_attn_b = d_attn.astype(jnp.bfloat16)
    grad_o = inner_left(attended_b, d_attn_b)
    d_attended = inner_right(d_attn_b, full_o).astype(jnp.bfloat16).reshape(TOK_DEV, HEADS, HD)
    d_probs = jnp.einsum("thd,kd->htk", d_attended, values_all, preferred_element_type=jnp.float32)
    row_total = jnp.sum(probs_f * d_probs, axis=-1, keepdims=True)
    d_scores = (probs_f * (d_probs - row_total)).astype(jnp.bfloat16)
    d_queries = (
        jnp.einsum("htk,kd->thd", d_scores, keys_all, preferred_element_type=jnp.float32) * factor
    )
    d_keys = (
        jnp.einsum("htk,thd->kd", d_scores, queries_b, preferred_element_type=jnp.float32) * factor
    )
    d_values = jnp.einsum("htk,thd->kd", probs_b, d_attended, preferred_element_type=jnp.float32)
    d_keys_own = d_keys[reach * TOK_DEV :]
    d_values_own = d_values[reach * TOK_DEV :]
    for distance in range(1, reach + 1):
        lower = (reach - distance) * TOK_DEV
        back_keys, back_values = (
            shifted(d_keys[lower : lower + TOK_DEV].astype(jnp.bfloat16), "seq", -distance).astype(
                jnp.float32
            ),
            shifted(
                d_values[lower : lower + TOK_DEV].astype(jnp.bfloat16), "seq", -distance
            ).astype(jnp.float32),
        )
        d_keys_own = d_keys_own + back_keys
        d_values_own = d_values_own + back_values
    d_q_raw, d_k_raw, d_gain_query, d_gain_key = pull_rot((d_queries, d_keys_own))
    d_q_b = d_q_raw.astype(jnp.bfloat16)
    d_k_b = d_k_raw.astype(jnp.bfloat16)
    d_v_b = d_values_own.astype(jnp.bfloat16)
    grad_q = inner_left(normed_b, d_q_b)
    grad_k = inner_left(normed_b, d_k_b)
    grad_v = inner_left(normed_b, d_v_b)
    d_normed = inner_right(d_q_b, full_q) + inner_right(d_k_b, full_k) + inner_right(d_v_b, full_v)
    d_from_in, d_gain_in = pull_in(d_normed)
    d_tokens = d_residual + d_from_in
    grad_gains = jnp.concatenate(
        [d_gain_in, d_gain_attn, d_gain_mlp, d_gain_out, d_gain_query, d_gain_key]
    )
    flat_terms = (
        grad_q.reshape(-1),
        grad_k.reshape(-1),
        grad_v.reshape(-1),
        grad_o.reshape(-1),
        grad_gate.reshape(-1),
        grad_up.reshape(-1),
        grad_down.reshape(-1),
        grad_gains,
    )
    reduced = (
        lax.psum_scatter(flat_terms[0], ("seq", "fsdp"), scatter_dimension=0, tiled=True),
        lax.psum_scatter(flat_terms[1], ("seq", "fsdp"), scatter_dimension=0, tiled=True),
        lax.psum_scatter(flat_terms[2], ("seq", "fsdp"), scatter_dimension=0, tiled=True),
        lax.psum_scatter(flat_terms[3], ("seq", "fsdp"), scatter_dimension=0, tiled=True),
        lax.psum_scatter(flat_terms[4], ("seq", "fsdp"), scatter_dimension=0, tiled=True),
        lax.psum_scatter(flat_terms[5], ("seq", "fsdp"), scatter_dimension=0, tiled=True),
        lax.psum_scatter(flat_terms[6], ("seq", "fsdp"), scatter_dimension=0, tiled=True),
        lax.psum_scatter(flat_terms[7], ("seq", "fsdp"), scatter_dimension=0, tiled=True),
    )
    return (
        output_b[None],
        d_tokens[None],
        reduced[0],
        reduced[1],
        reduced[2],
        reduced[3],
        reduced[4],
        reduced[5],
        reduced[6],
        reduced[7],
    )


def solution(mesh):
    in_specs = (
        P("fsdp", "seq", None),
        P(None, "fsdp"),
        P(None, "fsdp"),
        P(None, "fsdp"),
        P("fsdp", None),
        P(None, "fsdp"),
        P(None, "fsdp"),
        P("fsdp", None),
        P(),
        P("fsdp", "seq"),
        P("fsdp", "seq", None),
    )
    out_specs = (
        P("fsdp", "seq", None),
        P("fsdp", "seq", None),
        P(("seq", "fsdp")),
        P(("seq", "fsdp")),
        P(("seq", "fsdp")),
        P(("seq", "fsdp")),
        P(("seq", "fsdp")),
        P(("seq", "fsdp")),
        P(("seq", "fsdp")),
        P(("seq", "fsdp")),
    )
    return jax.shard_map(
        per_device, mesh=mesh, in_specs=in_specs, out_specs=out_specs, check_vma=False
    )
```

profile of v0, /device:TPU:0, one launch (start us, length us, event | category | flops | bytes accessed | tf_op | source)
XLA Modules:
  0.0 656.0 jit_solution(8187602211377042257)
XLA Ops:
  10.1 7.9 %all_gather.29 = bf16[640,256]{1,0:T(8,128)(2,1)S(1)} all-gather(bf16[640,128]{1,0:T(8,128)(2,1)S(1)} %copy-done.29), channel_id=1, replica_groups=mesh['seq'=16,'fsdp'=2] {'fsdp'}, dimensions={1}, use_global_device_ids=true | all-gather | bytes 491520 | tf_op jit(solution)/shard_map/all_gather | solution.py:76
  20.7 4.3 collective-permute-start.6
  25.0 4.4 collective-permute-start.5
  29.4 3.5 collective-permute-start.4
  32.9 7.0 %all_gather.28 = bf16[640,256]{1,0:T(8,128)(2,1)S(1)} all-gather(bf16[640,128]{1,0:T(8,128)(2,1)S(1)} %copy-done.30), channel_id=1, replica_groups=mesh['seq'=16,'fsdp'=2] {'fsdp'}, dimensions={1}, use_global_device_ids=true | all-gather | bytes 491520 | tf_op jit(solution)/shard_map/all_gather | solution.py:77
  42.4 4.0 collective-permute-start.2
  46.5 4.3 collective-permute-start.1
  50.8 3.4 collective-permute-start
  54.2 1.8 collective-permute-done
  56.2 1.8 copy.38
  60.6 5.3 all-gather.8.cloned.1.call-done
  65.9 1.8 multiply_reduce_fusion.10
  68.1 38.4 %all-gather.10.cloned.1.call-done = bf16[640,2048]{1,0:T(8,128)(2,1)} async-done(((bf16[640,1024]{1,0:T(8,128)(2,1)}), bf16[640,2048]{1,0:T(8,128)(2,1)}) %all-gather.10.cloned.1.call-update) | async-done | bytes 2621456 | tf_op jit(solution)/shard_map/all_gather | solution.py:79
  106.5 3.3 fusion.110
  109.8 37.2 %all-gather.12.cloned.1.call-done = bf16[640,2048]{1,0:T(8,128)(2,1)} async-done(((bf16[640,1024]{1,0:T(8,128)(2,1)}), bf16[640,2048]{1,0:T(8,128)(2,1)}) %all-gather.12.cloned.1.call-update) | async-done | bytes 2621456 | tf_op jit(solution)/shard_map/all_gather | solution.py:80
  147.0 3.8 multiply_convert_fusion.2
  150.8 36.6 %all-gather.14.cloned.1.call-done = bf16[2048,640]{1,0:T(8,128)(2,1)} async-done(((bf16[1024,640]{1,0:T(8,128)(2,1)}), bf16[2048,640]{1,0:T(8,128)(2,1)}) %all-gather.14.cloned.1.call-update) | async-done | bytes 2621456 | tf_op jit(solution)/shard_map/all_gather | solution.py:81
  187.4 2.6 multiply_reduce_fusion.8
  195.1 1.6 multiply_reduce_fusion.4
  204.3 3.2 convolution_bitcast_fusion
  207.5 3.3 convolution_bitcast_fusion.1
  210.7 3.1 fusion.114
  224.6 2.1 convolution_bitcast_fusion.2
  226.7 1.7 reshape.325
  228.4 4.0 copy.55
  232.4 6.1 copy.59
  238.5 3.6 copy.58
  242.1 6.5 reshape.328
  255.1 3.6 collective-permute-done.11
  264.6 48.2 %all-reduce.11 = f32[3072]{0:T(1024)S(1)} all-reduce(f32[3072]{0:T(1024)S(1)} %constant_dynamic-update-slice_fusion.11), channel_id=9, replica_groups=mesh['seq'=16,'fsdp'=2] {'seq','fsdp'}, use_global_device_ids=true, to_apply=%region_28.29.clone | all-reduce | flops 3072 | bytes 24576
  314.3 324.4 %all-reduce.15.cloned.1.call-done = (f32[655360]{0:T(1024)}, f32[163840]{0:T(1024)}, f32[163840]{0:T(1024)}, f32[655360]{0:T(1024)}, f32[1310720]{0:T(1024)}, /*index=5*/f32[1310720]{0:T(1024)}, f32[1310720]{0:T(1024)}) async-done(((f32[655360]{0:T(1024)}, f32[163840]{0:T(1024)}, f32[163840]{0:T(1024)}, f32[655360]{0:T(1024)}, f32[1310720]{0:T(1024)}, /*index=5*/f32[1310720]{0:T(1024)}, f32[1310720]{0:T(1024)}), ...) | async-done | bytes 22282256
  644.4 1.6 dynamic-slice.4
  (237 shorter events, 56.7 us)
Async XLA Ops:
  7.2 49.0 %all-gather.6.cloned.1.call-start = ((), (), s32[]{:S(2)}) async-start(), calls=%async_computation | async-start | bytes 1966080 | tf_op jit(solution)/shard_map/all_gather | solution.py:75
  7.9 58.0 %all-gather.8.cloned.1.call-start = ((), (), s32[]{:S(2)}) async-start(), calls=%async_computation.1 | async-start | bytes 1966080 | tf_op jit(solution)/shard_map/all_gather | solution.py:78
  8.7 97.8 %all-gather.10.cloned.1.call-start = ((), (), s32[]{:S(2)}) async-start(), calls=%async_computation.2 | async-start | bytes 3932160 | tf_op jit(solution)/shard_map/all_gather | solution.py:79
  9.4 137.5 %all-gather.12.cloned.1.call-start = ((), (), s32[]{:S(2)}) async-start(), calls=%async_computation.3 | async-start | bytes 3932160 | tf_op jit(solution)/shard_map/all_gather | solution.py:80
  10.0 177.4 %all-gather.14.cloned.1.call-start = ((), (), s32[]{:S(2)}) async-start(), calls=%async_computation.4 | async-start | bytes 3932160 | tf_op jit(solution)/shard_map/all_gather | solution.py:81
  17.9 22.9 %copy-start.14 = (bf16[640,256]{1,0:T(8,128)(2,1)}, bf16[640,256]{1,0:T(8,128)(2,1)S(1)}, u32[]{:S(2)}) copy-start(bf16[640,256]{1,0:T(8,128)(2,1)S(1)} %all_gather.29) | copy-start | bytes 983044
  18.7 23.5 %copy-start.41 = (f32[128]{0:T(128)}, f32[128]{0:T(128)S(1)}, u32[]{:S(2)}) copy-start(f32[128]{0:T(128)S(1)} %fusion.82) | copy-start | bytes 1540
  18.7 23.5 %copy-start.45 = (f32[128]{0:T(128)}, f32[128]{0:T(128)S(1)}, u32[]{:S(2)}) copy-start(f32[128]{0:T(128)S(1)} %get-tuple-element.62) | copy-start | bytes 1540
  18.7 23.5 %copy-start.32 = (f32[256]{0:T(256)}, f32[256]{0:T(256)S(1)}, u32[]{:S(2)}) copy-start(f32[256]{0:T(256)S(1)} %get-tuple-element.57) | copy-start | bytes 3076
  18.7 39.9 %copy-start.37 = (f32[256]{0:T(256)}, f32[256]{0:T(256)S(1)}, u32[]{:S(2)}) copy-start(f32[256]{0:T(256)S(1)} %get-tuple-element.56) | copy-start | bytes 3076
  19.4 39.4 %copy-start.23 = (f32[128,128]{1,0:T(8,128)}, f32[128,128]{1,0:T(8,128)S(1)}, u32[]{:S(2)}) copy-start(f32[128,128]{1,0:T(8,128)S(1)} %get-tuple-element.59) | copy-start | bytes 196612
  19.4 34.8 %collective-permute-start.7 = (bf16[128,256]{1,0:T(8,128)(2,1)S(1)}, bf16[128,256]{1,0:T(8,128)(2,1)S(1)}, u32[]{:S(2)}, u32[]{:S(2)}) collective-permute-start(bf16[128,256]{1,0:T(8,128)(2,1)S(1)} %pad_maximum_fusion.5), channel_id=1, source_target_pairs={{0,2},{2,4},{4,6},{6,8},{8,10},{10,12},{12,14},{14,16},{16,18},{18... | collective-permute-start | bytes 196616 | tf_op jit(solution)/shard_map/ppermute | solution.py:20
  20.7 30.1 %collective-permute-start.6 = (bf16[128,256]{1,0:T(8,128)(2,1)S(1)}, bf16[128,256]{1,0:T(8,128)(2,1)S(1)}, u32[]{:S(2)}, u32[]{:S(2)}) collective-permute-start(bf16[128,256]{1,0:T(8,128)(2,1)S(1)} %pad_maximum_fusion.5), channel_id=1, source_target_pairs={{0,4},{2,6},{4,8},{6,10},{8,12},{10,14},{12,16},{14,18},{16,20},{1... | collective-permute-start | bytes 196616 | tf_op jit(solution)/shard_map/ppermute | solution.py:20
  25.0 21.5 %collective-permute-start.5 = (bf16[128,256]{1,0:T(8,128)(2,1)S(1)}, bf16[128,256]{1,0:T(8,128)(2,1)S(1)}, u32[]{:S(2)}, u32[]{:S(2)}) collective-permute-start(bf16[128,256]{1,0:T(8,128)(2,1)S(1)} %pad_maximum_fusion.5), channel_id=1, source_target_pairs={{0,6},{2,8},{4,10},{6,12},{8,14},{10,16},{12,18},{14,20},{16,22},{... | collective-permute-start | bytes 196616 | tf_op jit(solution)/shard_map/ppermute | solution.py:20
  29.4 13.0 %collective-permute-start.4 = (bf16[128,256]{1,0:T(8,128)(2,1)S(1)}, bf16[128,256]{1,0:T(8,128)(2,1)S(1)}, u32[]{:S(2)}, u32[]{:S(2)}) collective-permute-start(bf16[128,256]{1,0:T(8,128)(2,1)S(1)} %pad_maximum_fusion.5), channel_id=1, source_target_pairs={{0,8},{2,10},{4,12},{6,14},{8,16},{10,18},{12,20},{14,22},{16,24},... | collective-permute-start | bytes 196616 | tf_op jit(solution)/shard_map/ppermute | solution.py:20
  40.8 15.3 %collective-permute-start.3 = (bf16[128,256]{1,0:T(8,128)(2,1)S(1)}, bf16[128,256]{1,0:T(8,128)(2,1)S(1)}, u32[]{:S(2)}, u32[]{:S(2)}) collective-permute-start(bf16[128,256]{1,0:T(8,128)(2,1)S(1)} %convolution_convert_fusion.2), channel_id=1, source_target_pairs={{0,2},{2,4},{4,6},{6,8},{8,10},{10,12},{12,14},{14,16},{16,18},{18... | collective-permute-start | bytes 196616 | tf_op jit(solution)/shard_map/ppermute | solution.py:20
  42.2 596.5 %all-reduce.15.cloned.1.call-start = ((), (), s32[]{:S(2)}) async-start(), calls=%async_computation.5 | async-start | bytes 44564480
  42.4 13.7 %collective-permute-start.2 = (bf16[128,256]{1,0:T(8,128)(2,1)S(1)}, bf16[128,256]{1,0:T(8,128)(2,1)S(1)}, u32[]{:S(2)}, u32[]{:S(2)}) collective-permute-start(bf16[128,256]{1,0:T(8,128)(2,1)S(1)} %convolution_convert_fusion.2), channel_id=1, source_target_pairs={{0,4},{2,6},{4,8},{6,10},{8,12},{10,14},{12,16},{14,18},{16,20},{1... | collective-permute-start | bytes 196616 | tf_op jit(solution)/shard_map/ppermute | solution.py:20
  46.5 9.6 %collective-permute-start.1 = (bf16[128,256]{1,0:T(8,128)(2,1)S(1)}, bf16[128,256]{1,0:T(8,128)(2,1)S(1)}, u32[]{:S(2)}, u32[]{:S(2)}) collective-permute-start(bf16[128,256]{1,0:T(8,128)(2,1)S(1)} %convolution_convert_fusion.2), channel_id=1, source_target_pairs={{0,6},{2,8},{4,10},{6,12},{8,14},{10,16},{12,18},{14,20},{16,22},{... | collective-permute-start | bytes 196616 | tf_op jit(solution)/shard_map/ppermute | solution.py:20
  50.8 5.2 collective-permute-start
  67.9 41.8 %copy-start.49 = (f32[128]{0:T(128)}, f32[128]{0:T(128)S(1)}, u32[]{:S(2)}) copy-start(f32[128]{0:T(128)S(1)} %get-tuple-element.30) | copy-start | bytes 1540
  150.8 39.2 %copy-start.3 = (bf16[128,2048]{1,0:T(8,128)(2,1)}, bf16[128,2048]{1,0:T(8,128)(2,1)S(1)}, u32[]{:S(2)}) copy-start(bf16[128,2048]{1,0:T(8,128)(2,1)S(1)} %get-tuple-element.72) | copy-start | bytes 1572868
  214.6 34.0 %collective-permute-start.12 = (bf16[128,256]{1,0:T(8,128)(2,1)}, bf16[128,256]{1,0:T(8,128)(2,1)S(1)}, u32[]{:S(2)}, u32[]{:S(2)}) collective-permute-start(bf16[128,256]{1,0:T(8,128)(2,1)} %get-tuple-element.40), channel_id=1, source_target_pairs={{2,0},{4,2},{6,4},{8,6},{10,8},{12,10},{14,12},{16,14},{18,16},{20... | collective-permute-start | bytes 196616 | tf_op jit(solution)/shard_map/ppermute | solution.py:20
  215.9 34.0 %collective-permute-start.15 = (bf16[128,256]{1,0:T(8,128)(2,1)}, bf16[128,256]{1,0:T(8,128)(2,1)}, u32[]{:S(2)}, u32[]{:S(2)}) collective-permute-start(bf16[128,256]{1,0:T(8,128)(2,1)} %get-tuple-element.41), channel_id=1, source_target_pairs={{8,0},{10,2},{12,4},{14,6},{16,8},{18,10},{20,12},{22,14},{24,16},... | collective-permute-start | bytes 196616 | tf_op jit(solution)/shard_map/ppermute | solution.py:20
  217.2 34.0 %collective-permute-start.14 = (bf16[128,256]{1,0:T(8,128)(2,1)}, bf16[128,256]{1,0:T(8,128)(2,1)}, u32[]{:S(2)}, u32[]{:S(2)}) collective-permute-start(bf16[128,256]{1,0:T(8,128)(2,1)} %get-tuple-element.42), channel_id=1, source_target_pairs={{6,0},{8,2},{10,4},{12,6},{14,8},{16,10},{18,12},{20,14},{22,16},{... | collective-permute-start | bytes 196616 | tf_op jit(solution)/shard_map/ppermute | solution.py:20
  218.5 34.0 %collective-permute-start.13 = (bf16[128,256]{1,0:T(8,128)(2,1)}, bf16[128,256]{1,0:T(8,128)(2,1)}, u32[]{:S(2)}, u32[]{:S(2)}) collective-permute-start(bf16[128,256]{1,0:T(8,128)(2,1)} %get-tuple-element.43), channel_id=1, source_target_pairs={{4,0},{6,2},{8,4},{10,6},{12,8},{14,10},{16,12},{18,14},{20,16},{2... | collective-permute-start | bytes 196616 | tf_op jit(solution)/shard_map/ppermute | solution.py:20
  223.3 31.8 %collective-permute-start.8 = (bf16[128,256]{1,0:T(8,128)(2,1)S(1)}, bf16[128,256]{1,0:T(8,128)(2,1)S(1)}, u32[]{:S(2)}, u32[]{:S(2)}) collective-permute-start(bf16[128,256]{1,0:T(8,128)(2,1)S(1)} %get-tuple-element.44), channel_id=1, source_target_pairs={{2,0},{4,2},{6,4},{8,6},{10,8},{12,10},{14,12},{16,14},{18,16},{20... | collective-permute-start | bytes 196616 | tf_op jit(solution)/shard_map/ppermute | solution.py:20
  248.6 10.2 %collective-permute-start.11 = (bf16[128,256]{1,0:T(8,128)(2,1)S(1)}, bf16[128,256]{1,0:T(8,128)(2,1)S(1)}, u32[]{:S(2)}, u32[]{:S(2)}) collective-permute-start(bf16[128,256]{1,0:T(8,128)(2,1)S(1)} %get-tuple-element.45), channel_id=1, source_target_pairs={{8,0},{10,2},{12,4},{14,6},{16,8},{18,10},{20,12},{22,14},{24,16},... | collective-permute-start | bytes 196616 | tf_op jit(solution)/shard_map/ppermute | solution.py:20
  249.9 8.9 %collective-permute-start.10 = (bf16[128,256]{1,0:T(8,128)(2,1)S(1)}, bf16[128,256]{1,0:T(8,128)(2,1)S(1)}, u32[]{:S(2)}, u32[]{:S(2)}) collective-permute-start(bf16[128,256]{1,0:T(8,128)(2,1)S(1)} %get-tuple-element.46), channel_id=1, source_target_pairs={{6,0},{8,2},{10,4},{12,6},{14,8},{16,10},{18,12},{20,14},{22,16},{... | collective-permute-start | bytes 196616 | tf_op jit(solution)/shard_map/ppermute | solution.py:20
  251.2 7.6 %collective-permute-start.9 = (bf16[128,256]{1,0:T(8,128)(2,1)S(1)}, bf16[128,256]{1,0:T(8,128)(2,1)S(1)}, u32[]{:S(2)}, u32[]{:S(2)}) collective-permute-start(bf16[128,256]{1,0:T(8,128)(2,1)S(1)} %get-tuple-element.47), channel_id=1, source_target_pairs={{4,0},{6,2},{8,4},{10,6},{12,8},{14,10},{16,12},{18,14},{20,16},{2... | collective-permute-start | bytes 196616 | tf_op jit(solution)/shard_map/ppermute | solution.py:20
  263.8 49.6 %copy-start.48 = (f32[128]{0:T(128)S(1)}, f32[128]{0:T(128)}, u32[]{:S(2)}) copy-start(f32[128]{0:T(128)} %copy-done.47) | copy-start | bytes 1540
  263.8 49.6 %copy-start.9 = (f32[128,640]{1,0:T(8,128)S(1)}, f32[128,640]{1,0:T(8,128)}, u32[]{:S(2)}) copy-start(f32[128,640]{1,0:T(8,128)} %copy-done.8) | copy-start | bytes 983044
  (46 other events, 211.3 us)
Sparse Core Ops, SparseCore 0:
  9.6 27.6 all-gather.5
  38.8 27.0 all-gather.7
  67.4 39.0 all-gather.9
  107.9 39.0 all-gather.11
  148.4 39.0 all-gather.13
  262.0 376.6 all-reduce.14
where the time goes:
time: 657 us; the launch traced here: 656 us
  waiting for transfers between devices  450 us (68%)
  blocking collectives  63 us (10%)
  local copies, waits for them, and re-layouts  46.6 us (7%)
  starting transfers between devices  37.1 us (6%)
  matrix products  35.4 us (5%)
  between operations  15.2 us (2%)
  other arithmetic  8.64 us (1%)
    unnamed x7, waiting for transfers between devices  327 us
    unnamed x1, blocking collectives  48.2 us
    all_gather x1, waiting for transfers between devices, per_device(): lax.all_gather(w_gate, 'fsdp', axis=1, tiled=True)  38.4 us
    all_gather x1, waiting for transfers between devices, per_device(): lax.all_gather(w_up, 'fsdp', axis=1, tiled=True)  37.2 us
    ppermute x16, starting transfers between devices, shifted(): lax.ppermute(value, axis, [(source, source + steps) for source in range(l...  36.9 us
    all_gather x1, waiting for transfers between devices, per_device(): lax.all_gather(w_down, 'fsdp', axis=0, tiled=True)  36.6 us
    unnamed x138, local copies, waits for them, and re-layouts  33.8 us
  transfers between devices with their start and end apart: 22, of which 7 were waited for; matrix products, arithmetic and copies ran while one was open for 7% of the time, Pallas kernels for 0%

commit v1 on v0

v1 whole, which is shorter than its diff:
```python
import jax
import jax.numpy as jnp
from jax import lax
from jax.sharding import PartitionSpec as P

D = 640
HEADS = 4
HD = 256
WINDOW = 512
TOK_DEV = 128


EPSILON = 1e-06
NEGATIVE = -1e30


def shifted(value, axis, steps):
    count = lax.axis_size(axis)
    leading, last = (max(0, -steps), min(count, count - steps))
    return lax.ppermute(value, axis, [(source, source + steps) for source in range(leading, last)])


def rms_norm(vector, gain_vec):
    return (
        vector * lax.rsqrt(jnp.mean(vector * vector, axis=-1, keepdims=True) + EPSILON) * gain_vec
    )


def rotate(vector, places):
    half_size = vector.shape[-1] // 2
    inverse = 10000.0 ** (-2.0 * jnp.arange(half_size, dtype=jnp.float32) / vector.shape[-1])
    angles = places.astype(jnp.float32)[:, None] * inverse[None, :]
    cosine = jnp.cos(angles)
    sine_part = jnp.sin(angles)
    if vector.ndim == 3:
        cosine = cosine[:, None, :]
        sine_part = sine_part[:, None, :]
    first_half = vector[..., :half_size]
    second = vector[..., half_size:]
    return jnp.concatenate(
        [first_half * cosine - second * sine_part, second * cosine + first_half * sine_part],
        axis=-1,
    )


def queries_keys(q_raw, k_raw, gain_query, gain_key, places):
    queries = rotate(rms_norm(q_raw.reshape(q_raw.shape[0], q_raw.shape[1] // HD, HD), gain_query), places)
    return (queries, rotate(rms_norm(k_raw, gain_key), places))


def gelu_mix(gate_raw, up_raw):
    return jax.nn.gelu(gate_raw, approximate=True) * up_raw


def matmul(left_side, right_side):
    return jnp.dot(left_side, right_side, preferred_element_type=jnp.float32)


def inner_left(left_side, right_side):
    return lax.dot_general(
        left_side, right_side, (((0,), (0,)), ((), ())), preferred_element_type=jnp.float32
    )


def inner_right(left_side, right_side):
    return lax.dot_general(
        left_side, right_side, (((1,), (1,)), ((), ())), preferred_element_type=jnp.float32
    )


def swapped(value):
    return lax.ppermute(value, "fsdp", [(0, 1), (1, 0)])


def pair_sum(partial):
    half = partial.shape[0] // 2
    far = swapped(partial.astype(jnp.bfloat16)).astype(jnp.float32)
    return partial + jnp.concatenate([far[half:], far[:half]], axis=0)


def flat_rows(piece, fsdp):
    other = swapped(piece)
    whole = jnp.where(
        fsdp == 0,
        jnp.concatenate([piece, other], axis=1),
        jnp.concatenate([other, piece], axis=1),
    ).reshape(2, -1)
    return lax.dynamic_index_in_dim(whole, fsdp, 0, keepdims=False)


def reduce_generic(columns, rows, fsdp):
    count = lax.axis_size("seq")
    packed = jnp.concatenate(
        [value.astype(jnp.bfloat16).reshape(count, -1) for value in columns + rows], axis=1
    )
    mine = lax.psum_scatter(packed, "seq", scatter_dimension=0, tiled=True)
    mine = mine.astype(jnp.float32).reshape(-1)
    results = []
    start = 0
    for value in columns:
        size = value.size // count
        piece = mine[start : start + size].reshape(-1, value.shape[1])
        results.append(flat_rows(piece, fsdp))
        start += size
    moves = []
    for plane in range(2):
        for chunk in range(count):
            target = (count // 2) * plane + chunk // 2
            moves.append((chunk * 2 + plane, target * 2 + chunk % 2))
    for value in rows:
        size = value.size // count
        results.append(lax.ppermute(mine[start : start + size], ("seq", "fsdp"), moves))
        start += size
    return results


def per_device(tokens, w_q, w_k, w_v, w_o, w_gate, w_up, w_down, gains, positions, cotangent):
    fsdp = lax.axis_index("fsdp")
    block = tokens.shape[1]
    own_pack = jnp.concatenate([tokens[0], cotangent[0]], axis=0)
    far_pack = swapped(own_pack)
    w_kv = jnp.concatenate([w_k, w_v], axis=1)
    far_kv = swapped(w_kv)
    half = w_k.shape[1]

    def widened(near, far):
        return jnp.where(
            fsdp == 0,
            jnp.concatenate([near, far], axis=1),
            jnp.concatenate([far, near], axis=1),
        )

    full_k = widened(w_kv[:, :half], far_kv[:, :half])
    full_v = widened(w_kv[:, half:], far_kv[:, half:])
    far_places = swapped(positions)
    places2 = jnp.concatenate([positions, far_places], axis=0)
    places = places2.reshape(-1)
    tokens_f = jnp.concatenate([tokens[0], far_pack[:block]], axis=0).astype(jnp.float32)
    d_out = jnp.concatenate([cotangent[0], far_pack[block:]], axis=0).astype(jnp.float32)
    gain_in = gains[0:D]
    gain_attn = gains[D : 2 * D]
    gain_mlp = gains[2 * D : 3 * D]
    gain_out = gains[3 * D : 4 * D]
    gain_query = gains[4 * D : 4 * D + HD]
    gain_key = gains[4 * D + HD : 4 * D + 2 * HD]
    normed = rms_norm(tokens_f, gain_in)
    normed_b = normed.astype(jnp.bfloat16)
    q_raw = matmul(normed_b, w_q)
    k_raw = matmul(normed_b, full_k)
    v_raw = matmul(normed_b, full_v)

    def rotary(q_part, k_part, gq_part, gk_part):
        return queries_keys(q_part, k_part, gq_part, gk_part, places)

    (queries, keys_own), pull_rot = jax.vjp(rotary, q_raw, k_raw, gain_query, gain_key)
    heads = queries.shape[1]
    queries_b = queries.astype(jnp.bfloat16).reshape(2, block, heads, HD)
    kv_b = jnp.concatenate([keys_own, v_raw], axis=1).astype(jnp.bfloat16)
    kv_b = kv_b.reshape(2, block, 2 * HD)
    reach = WINDOW // block
    parts = [shifted(kv_b, "seq", distance) for distance in range(reach, 0, -1)]
    kv_all = jnp.concatenate(parts + [kv_b], axis=1)
    keys_all = kv_all[:, :, :HD]
    values_all = kv_all[:, :, HD:]
    span = (reach + 1) * block
    row_ids = jnp.arange(block, dtype=jnp.int32)[:, None]
    col_ids = jnp.arange(span, dtype=jnp.int32)[None, :]
    offsets = row_ids - col_ids + reach * block
    first_key = (lax.axis_index("seq") - reach) * block
    allowed = (
        (offsets >= 0)[None]
        & (offsets[None] <= jnp.minimum(places2[:, :, None], WINDOW - 1))
        & (first_key + col_ids >= 0)[None]
    )
    factor = HD ** (-0.5)
    raw_scores = (
        jnp.einsum("bthd,bkd->bhtk", queries_b, keys_all, preferred_element_type=jnp.float32)
        * factor
    )
    scores = jnp.where(allowed[:, None], raw_scores, NEGATIVE)
    exponent = jnp.exp(scores - jnp.max(scores, axis=-1, keepdims=True))
    probs_f = exponent / jnp.sum(exponent, axis=-1, keepdims=True)
    probs_b = probs_f.astype(jnp.bfloat16)
    attended = jnp.einsum(
        "bhtk,bkd->bthd", probs_b, values_all, preferred_element_type=jnp.float32
    )
    attended_b = attended.reshape(2 * block, heads * HD).astype(jnp.bfloat16)
    attn_raw = pair_sum(matmul(attended_b, w_o))
    attn_normed, pull_attn = jax.vjp(rms_norm, attn_raw, gain_attn)
    residual = tokens_f + attn_normed
    ffn_in, pull_mlp = jax.vjp(rms_norm, residual, gain_mlp)
    ffn_b = ffn_in.astype(jnp.bfloat16)
    gate_raw = matmul(ffn_b, w_gate)
    up_raw = matmul(ffn_b, w_up)
    hidden, pull_mix = jax.vjp(gelu_mix, gate_raw, up_raw)
    hidden_b = hidden.astype(jnp.bfloat16)
    down_raw = pair_sum(matmul(hidden_b, w_down))
    down_normed, pull_out = jax.vjp(rms_norm, down_raw, gain_out)
    output_b = (residual[:block] + down_normed[:block]).astype(jnp.bfloat16)
    d_down, d_gain_out = pull_out(d_out)
    d_down_b = d_down.astype(jnp.bfloat16)
    grad_down = inner_left(hidden_b, d_down_b)
    d_hidden = inner_right(d_down_b, w_down)
    d_gate, d_up = pull_mix(d_hidden)
    d_gate_b = d_gate.astype(jnp.bfloat16)
    d_up_b = d_up.astype(jnp.bfloat16)
    d_ffn = pair_sum(inner_right(d_gate_b, w_gate) + inner_right(d_up_b, w_up))
    grad_gate = inner_left(ffn_b, d_gate_b)
    grad_up = inner_left(ffn_b, d_up_b)
    d_from_mlp, d_gain_mlp = pull_mlp(d_ffn)
    d_residual = d_out + d_from_mlp
    d_attn, d_gain_attn = pull_attn(d_residual)
    d_attn_b = d_attn.astype(jnp.bfloat16)
    grad_o = inner_left(attended_b, d_attn_b)
    d_attended = inner_right(d_attn_b, w_o).astype(jnp.bfloat16).reshape(2, block, heads, HD)
    d_probs = jnp.einsum(
        "bthd,bkd->bhtk", d_attended, values_all, preferred_element_type=jnp.float32
    )
    row_total = jnp.sum(probs_f * d_probs, axis=-1, keepdims=True)
    d_scores = (probs_f * (d_probs - row_total)).astype(jnp.bfloat16)
    d_keys = (
        jnp.einsum("bhtk,bthd->bkd", d_scores, queries_b, preferred_element_type=jnp.float32)
        * factor
    )
    d_values = jnp.einsum(
        "bhtk,bthd->bkd", probs_b, d_attended, preferred_element_type=jnp.float32
    )
    d_kv = jnp.concatenate([d_keys, d_values], axis=2)
    d_kv_far = d_kv[:, : reach * block].astype(jnp.bfloat16)
    d_kv_own = d_kv[:, reach * block :]
    for distance in range(1, reach + 1):
        lower = (reach - distance) * block
        d_kv_own = d_kv_own + shifted(
            d_kv_far[:, lower : lower + block], "seq", -distance
        ).astype(jnp.float32)
    d_kv_own = pair_sum(d_kv_own).reshape(2 * block, 2 * HD)
    d_queries = (
        jnp.einsum("bhtk,bkd->bthd", d_scores, keys_all, preferred_element_type=jnp.float32)
        * factor
    ).reshape(2 * block, heads, HD)
    d_q_raw, d_k_raw, d_gain_query, d_gain_key = pull_rot((d_queries, d_kv_own[:, :HD]))
    d_q_b = d_q_raw.astype(jnp.bfloat16)
    d_kv_b = jnp.concatenate([d_k_raw, d_kv_own[:, HD:]], axis=1).astype(jnp.bfloat16)
    from_q = inner_right(d_q_b, w_q)
    far_q = swapped(from_q[block:].astype(jnp.bfloat16)).astype(jnp.float32)
    grad_q = inner_left(normed_b, d_q_b)
    d_k_half = lax.dynamic_slice_in_dim(d_kv_b[:, :HD], fsdp * half, half, 1)
    d_v_half = lax.dynamic_slice_in_dim(d_kv_b[:, HD:], fsdp * half, half, 1)
    grad_k = inner_left(normed_b, d_k_half)
    grad_v = inner_left(normed_b, d_v_half)
    d_normed = (
        from_q[:block]
        + far_q
        + inner_right(d_kv_b[:block, :HD], full_k)
        + inner_right(d_kv_b[:block, HD:], full_v)
    )
    d_from_in, d_gain_in = jax.vjp(rms_norm, tokens_f[:block], gain_in)[1](d_normed)
    d_tokens = d_residual[:block] + d_from_in
    grad_gains = jnp.concatenate(
        [
            d_gain_in,
            0.5 * d_gain_attn,
            0.5 * d_gain_mlp,
            0.5 * d_gain_out,
            d_gain_query,
            0.5 * d_gain_key,
        ]
    )
    flat_gate, flat_up, flat_down = reduce_generic([grad_gate, grad_up], [grad_down], fsdp)
    flat_q, flat_k, flat_v, flat_o = reduce_generic([grad_q, grad_k, grad_v], [grad_o], fsdp)
    flat_gains = lax.psum_scatter(
        grad_gains, ("seq", "fsdp"), scatter_dimension=0, tiled=True
    )
    return (
        output_b[None],
        d_tokens[None],
        flat_q,
        flat_k,
        flat_v,
        flat_o,
        flat_gate,
        flat_up,
        flat_down,
        flat_gains,
    )


def solution(mesh):
    in_specs = (
        P("fsdp", "seq", None),
        P(None, "fsdp"),
        P(None, "fsdp"),
        P(None, "fsdp"),
        P("fsdp", None),
        P(None, "fsdp"),
        P(None, "fsdp"),
        P("fsdp", None),
        P(),
        P("fsdp", "seq"),
        P("fsdp", "seq", None),
    )
    out_specs = (
        P("fsdp", "seq", None),
        P("fsdp", "seq", None),
        P(("seq", "fsdp")),
        P(("seq", "fsdp")),
        P(("seq", "fsdp")),
        P(("seq", "fsdp")),
        P(("seq", "fsdp")),
        P(("seq", "fsdp")),
        P(("seq", "fsdp")),
        P(("seq", "fsdp")),
    )
    return jax.shard_map(
        per_device, mesh=mesh, in_specs=in_specs, out_specs=out_specs, check_vma=False
    )
```

time: 657 us -> 319 us (0.49)
  waiting for transfers between devices: 450 us -> 129 us
  blocking collectives: 63 us -> 45.4 us
  other arithmetic: 8.64 us -> 24.8 us
  local copies, waits for them, and re-layouts: 46.6 us -> 36.9 us
  matrix products: 35.4 us -> 25.7 us
    unnamed x7 -> x2, waiting for transfers between devices: 327 us -> 77.8 us
    all_gather x5 -> x0, waiting for transfers between devices: 118 us -> none  [the longest x1 38.4 us: per_device(): lax.all_gather(w_gate, 'fsdp', axis=1, tiled=True)]
    ppermute x0 -> x15, waiting for transfers between devices: none -> 42.1 us  [the longest x13 42.1 us: swapped(): return lax.ppermute(value, 'fsdp', [(0, 1), (1, 0)])]
    ppermute x0 -> x15, starting transfers between devices: none -> 21.2 us  [the longest x13 19.7 us: swapped(): return lax.ppermute(value, 'fsdp', [(0, 1), (1, 0)])]
    ppermute x16 -> x8, starting transfers between devices: 36.9 us -> 18.9 us  [shifted(): lax.ppermute(value, axis, [(source, source + steps) for source in range(l...]
    unnamed x138 -> x165, local copies, waits for them, and re-layouts: 33.8 us -> 16.3 us
    all_gather x2 -> x0, blocking collectives: 14.8 us -> none  [the longest x1 7.86 us: per_device(): lax.all_gather(w_k, 'fsdp', axis=1, tiled=True)]
    concatenate x2 -> x7, other arithmetic: 0.02 us -> 7.71 us  [the longest x2 4.76 us: reduce_generic(): jnp.concatenate([value.astype(jnp.bfloat16).reshape(count, -1) for value...]
  transfers between devices with their start and end apart: 22 -> 24, of which waited for: 7 -> 11; matrix products, arithmetic and copies ran while one was open for 7% -> 12% of each run, Pallas kernels for 0% -> 0%
where the time goes in v1:
time: 319 us; the launch traced here: 317 us
  waiting for transfers between devices  129 us (40%)
  blocking collectives  45.4 us (14%)
  starting transfers between devices  40.2 us (13%)
  local copies, waits for them, and re-layouts  36.9 us (12%)
  matrix products  25.7 us (8%)
  other arithmetic  24.8 us (8%)
  between operations  15.4 us (5%)
    unnamed x2, waiting for transfers between devices  77.8 us
    unnamed x1, blocking collectives  45.4 us
    ppermute x13, waiting for transfers between devices, swapped(): return lax.ppermute(value, 'fsdp', [(0, 1), (1, 0)])  42.1 us
    ppermute x13, starting transfers between devices, swapped(): return lax.ppermute(value, 'fsdp', [(0, 1), (1, 0)])  19.7 us
    ppermute x8, starting transfers between devices, shifted(): lax.ppermute(value, axis, [(source, source + steps) for source in range(l...  18.9 us
    unnamed x165, local copies, waits for them, and re-layouts  16.3 us
    reshape x7, local copies, waits for them, and re-layouts, reduce_generic(): value.astype(jnp.bfloat16).reshape(count, -1)  9.6 us
    ppermute x8, waiting for transfers between devices, shifted(): lax.ppermute(value, axis, [(source, source + steps) for source in range(l...  9.1 us
  transfers between devices with their start and end apart: 24, of which 11 were waited for; matrix products, arithmetic and copies ran while one was open for 12% of the time, Pallas kernels for 0%

profile of v1, /device:TPU:0, one launch (start us, length us, event | category | flops | bytes accessed | tf_op | source)
XLA Modules:
  0.0 317.4 jit_solution(7069090854022979884)
XLA Ops:
  8.4 3.0 collective-permute-start
  12.5 2.0 collective-permute-start.2
  14.7 11.5 %collective-permute-done.2 = s32[1,128]{1,0:T(1,128)S(1)} collective-permute-done((s32[1,128]{1,0:T(1,128)S(1)}, s32[1,128]{1,0:T(1,128)S(1)}, u32[]{:S(2)}, u32[]{:S(2)}) %collective-permute-start.2) | collective-permute-done | bytes 544 | tf_op jit(solution)/shard_map/ppermute | solution.py:72
  31.9 4.4 %collective-permute-start.3 = (bf16[2,128,512]{2,1,0:T(8,128)(2,1)}, bf16[2,128,512]{2,1,0:T(8,128)(2,1)}, u32[]{:S(2)}, u32[]{:S(2)}) collective-permute-start(bf16[2,128,512]{2,1,0:T(8,128)(2,1)} %pad_maximum_fusion.9), channel_id=1, source_target_pairs={{0,8},{2,10},{4,12},{6,14},{8,16},{10,18},{12,20},{14,22},{16,24},... | collective-permute-start | bytes 786440 | tf_op jit(solution)/shard_map/ppermute | solution.py:20
  36.3 2.3 collective-permute-start.4
  38.7 3.8 %collective-permute-start.5 = (bf16[2,128,512]{2,1,0:T(8,128)(2,1)}, bf16[2,128,512]{2,1,0:T(8,128)(2,1)}, u32[]{:S(2)}, u32[]{:S(2)}) collective-permute-start(bf16[2,128,512]{2,1,0:T(8,128)(2,1)} %pad_maximum_fusion.9), channel_id=1, source_target_pairs={{0,4},{2,6},{4,8},{6,10},{8,12},{10,14},{12,16},{14,18},{16,20},{1... | collective-permute-start | bytes 786440 | tf_op jit(solution)/shard_map/ppermute | solution.py:20
  42.5 3.2 %collective-permute-start.6 = (bf16[2,128,512]{2,1,0:T(8,128)(2,1)}, bf16[2,128,512]{2,1,0:T(8,128)(2,1)}, u32[]{:S(2)}, u32[]{:S(2)}) collective-permute-start(bf16[2,128,512]{2,1,0:T(8,128)(2,1)} %pad_maximum_fusion.9), channel_id=1, source_target_pairs={{0,2},{2,4},{4,6},{6,8},{8,10},{10,12},{12,14},{14,16},{16,18},{18... | collective-permute-start | bytes 786440 | tf_op jit(solution)/shard_map/ppermute | solution.py:20
  53.0 1.9 fusion.105
  56.0 2.2 fusion.8
  59.8 1.6 collective-permute-start.7
  61.4 8.8 %collective-permute-done.7 = bf16[256,640]{1,0:T(8,128)(2,1)S(1)} collective-permute-done((bf16[256,640]{1,0:T(8,128)(2,1)S(1)}, bf16[256,640]{1,0:T(8,128)(2,1)S(1)}, u32[]{:S(2)}, u32[]{:S(2)}) %collective-permute-start.7) | collective-permute-done | bytes 327712 | tf_op jit(solution)/shard_map/ppermute | solution.py:72
  73.1 1.7 multiply_convert_fusion.2
  80.5 5.6 %collective-permute-done.8 = bf16[256,640]{1,0:T(8,128)(2,1)} collective-permute-done((bf16[256,640]{1,0:T(8,128)(2,1)}, bf16[256,640]{1,0:T(8,128)(2,1)}, u32[]{:S(2)}, u32[]{:S(2)}) %collective-permute-start.8) | collective-permute-done | bytes 327712 | tf_op jit(solution)/shard_map/ppermute | solution.py:72
  88.6 1.7 convolution_convert_fusion
  92.2 1.6 convolution_convert_fusion.2
  93.9 1.6 convolution_convert_fusion.1
  97.7 2.6 reshape.376
  100.3 2.5 reshape.375
  102.8 2.6 reshape.374
  105.4 3.5 %pad_maximum_fusion = bf16[16,122880]{1,0:T(8,128)(2,1)} fusion(bf16[16,40960]{1,0:T(8,128)(2,1)} %reshape.376, bf16[16,40960]{1,0:T(8,128)(2,1)} %reshape.375, bf16[16,40960]{1,0:T(8,128)(2,1)} %reshape.374), kind=kLoop, calls=%fused_computation.1 | loop fusion | flops 11796480 | bytes 7864320 | tf_op jit(solution)/shard_map/concatenate | solution.py:93
  112.5 1.9 convolution_bitcast_fusion
  123.7 2.2 collective-permute-done.14
  127.2 5.6 %collective-permute-done.12 = bf16[2,128,512]{1,2,0:T(8,128)(2,1)S(1)} collective-permute-done((bf16[2,128,512]{1,2,0:T(8,128)(2,1)S(1)}, bf16[2,128,512]{1,2,0:T(8,128)(2,1)S(1)}, u32[]{:S(2)}, u32[]{:S(2)}) %collective-permute-start.12) | collective-permute-done | bytes 262176 | tf_op jit(solution)/shard_map/ppermute | solution.py:20
  137.9 3.7 %collective-permute-done.15 = bf16[2,128,512]{1,2,0:T(8,128)(2,1)S(1)} collective-permute-done((bf16[2,128,512]{1,2,0:T(8,128)(2,1)}, bf16[2,128,512]{1,2,0:T(8,128)(2,1)S(1)}, u32[]{:S(2)}, u32[]{:S(2)}) %collective-permute-start.15) | collective-permute-done | bytes 262176 | tf_op jit(solution)/shard_map/ppermute | solution.py:72
  150.2 5.8 %collective-permute-done.10 = bf16[128,640]{1,0:T(8,128)(2,1)S(1)} collective-permute-done((bf16[128,640]{1,0:T(8,128)(2,1)S(1)}, bf16[128,640]{1,0:T(8,128)(2,1)S(1)}, u32[]{:S(2)}, u32[]{:S(2)}) %collective-permute-start.10) | collective-permute-done | bytes 163872 | tf_op jit(solution)/shard_map/ppermute | solution.py:72
  157.3 45.4 %all-reduce.6 = f32[3072]{0:T(1024)S(1)} all-reduce(f32[3072]{0:T(1024)S(1)} %constant_dynamic-update-slice_fusion.6), channel_id=4, replica_groups=mesh['seq'=16,'fsdp'=2] {'seq','fsdp'}, use_global_device_ids=true, to_apply=%region_24.25.clone | all-reduce | flops 3072 | bytes 24576
  204.2 77.8 %all-reduce.10.cloned.1.call-done = (bf16[16,51200]{1,0:T(8,128)(2,1)}, bf16[16,122880]{1,0:T(8,128)(2,1)}) async-done(((bf16[16,51200]{1,0:T(8,128)(2,1)}, bf16[16,122880]{1,0:T(8,128)(2,1)}), (bf16[16,51200]{1,0:T(8,128)(2,1)}, bf16[16,122880]{1,0:T(8,128)(2,1)})) %all-reduce.10.cloned.1.call-update) | async-done | bytes 5570576
  282.0 2.0 dynamic-slice_convert_fusion.1
  288.7 2.6 dynamic-slice_convert_fusion
  292.1 5.0 %collective-permute-start.20 = (f32[40,1024]{1,0:T(8,128)S(1)}, f32[40,1024]{1,0:T(8,128)S(1)}, u32[]{:S(2)}, u32[]{:S(2)}) collective-permute-start(f32[40,1024]{1,0:T(8,128)S(1)} %reshape.377), channel_id=1, source_target_pairs={{0,1},{1,0},{2,3},{3,2},{4,5},{5,4},{6,7},{7,6},{8,9},{9,8},{10,11... | collective-permute-start | bytes 491528 | tf_op jit(solution)/shard_map/ppermute | solution.py:72
  300.2 2.4 collective-permute-done.20
  302.5 4.5 %collective-permute-done.21 = f32[40,1024]{1,0:T(8,128)S(1)} collective-permute-done((f32[40,1024]{1,0:T(8,128)S(1)}, f32[40,1024]{1,0:T(8,128)S(1)}, u32[]{:S(2)}, u32[]{:S(2)}) %collective-permute-start.21) | collective-permute-done | bytes 163872 | tf_op jit(solution)/shard_map/ppermute | solution.py:72
  (315 shorter events, 75.2 us)
Async XLA Ops:
  7.2 67.6 %copy-start = (bf16[1024,640]{1,0:T(8,128)(2,1)S(1)}, bf16[1024,640]{1,0:T(8,128)(2,1)}, u32[]{:S(2)}) copy-start(bf16[1024,640]{1,0:T(8,128)(2,1)} %param.18) | copy-start | bytes 3932164
  7.2 274.7 %all-reduce.10.cloned.1.call-start = ((), (), s32[]{:S(2)}) async-start(), calls=%async_computation | async-start | bytes 11141120
  8.4 19.4 %copy-start.10 = (bf16[1,128,640]{2,1,0:T(8,128)(2,1)S(1)}, bf16[1,128,640]{2,1,0:T(8,128)(2,1)}, u32[]{:S(2)}) copy-start(bf16[1,128,640]{2,1,0:T(8,128)(2,1)} %param.11) | copy-start | bytes 491524
  8.4 18.7 %collective-permute-start = (bf16[256,640]{1,0:T(8,128)(2,1)S(1)}, bf16[256,640]{1,0:T(8,128)(2,1)S(1)}, u32[]{:S(2)}, u32[]{:S(2)}) collective-permute-start(bf16[256,640]{1,0:T(8,128)(2,1)S(1)} %pad_maximum_fusion.3), channel_id=1, source_target_pairs={{0,1},{1,0},{2,3},{3,2},{4,5},{5,4},{6,7},{7,6},{8,9},{9,8},{10,11... | collective-permute-start | bytes 983048 | tf_op jit(solution)/shard_map/ppermute | solution.py:72
  12.5 15.5 %collective-permute-start.1 = (bf16[640,256]{1,0:T(8,128)(2,1)S(1)}, bf16[640,256]{1,0:T(8,128)(2,1)S(1)}, u32[]{:S(2)}, u32[]{:S(2)}) collective-permute-start(bf16[640,256]{1,0:T(8,128)(2,1)S(1)} %pad_maximum_fusion.6), channel_id=1, source_target_pairs={{0,1},{1,0},{2,3},{3,2},{4,5},{5,4},{6,7},{7,6},{8,9},{9,8},{10,11... | collective-permute-start | bytes 983048 | tf_op jit(solution)/shard_map/ppermute | solution.py:72
  12.5 13.7 %collective-permute-start.2 = (s32[1,128]{1,0:T(1,128)S(1)}, s32[1,128]{1,0:T(1,128)S(1)}, u32[]{:S(2)}, u32[]{:S(2)}) collective-permute-start(s32[1,128]{1,0:T(1,128)S(1)} %copy-done.74), channel_id=1, source_target_pairs={{0,1},{1,0},{2,3},{3,2},{4,5},{5,4},{6,7},{7,6},{8,9},{9,8},{10,11... | collective-permute-start | bytes 1544 | tf_op jit(solution)/shard_map/ppermute | solution.py:72
  14.6 31.1 %copy-start.62 = (f32[640]{0:T(1024)}, f32[640]{0:T(1024)S(1)}, u32[]{:S(2)}) copy-start(f32[640]{0:T(1024)S(1)} %get-tuple-element.70) | copy-start | bytes 7684
  14.6 32.4 %copy-start.64 = (f32[256]{0:T(256)}, f32[256]{0:T(256)S(1)}, u32[]{:S(2)}) copy-start(f32[256]{0:T(256)S(1)} %get-tuple-element.72) | copy-start | bytes 3076
  27.8 42.7 %copy-start.12 = (bf16[128,640]{1,0:T(8,128)(2,1)}, bf16[128,640]{1,0:T(8,128)(2,1)S(1)}, u32[]{:S(2)}) copy-start(bf16[128,640]{1,0:T(8,128)(2,1)S(1)} %get-tuple-element.58) | copy-start | bytes 491524
  27.9 17.8 %copy-start.72 = (f32[256]{0:T(256)}, f32[256]{0:T(256)S(1)}, u32[]{:S(2)}) copy-start(f32[256]{0:T(256)S(1)} %add_rsqrt_fusion) | copy-start | bytes 3076
  29.9 16.2 %copy-start.68 = (f32[256]{0:T(256)}, f32[256]{0:T(256)S(1)}, u32[]{:S(2)}) copy-start(f32[256]{0:T(256)S(1)} %get-tuple-element.82) | copy-start | bytes 3076
  31.9 16.0 %collective-permute-start.3 = (bf16[2,128,512]{2,1,0:T(8,128)(2,1)}, bf16[2,128,512]{2,1,0:T(8,128)(2,1)}, u32[]{:S(2)}, u32[]{:S(2)}) collective-permute-start(bf16[2,128,512]{2,1,0:T(8,128)(2,1)} %pad_maximum_fusion.9), channel_id=1, source_target_pairs={{0,8},{2,10},{4,12},{6,14},{8,16},{10,18},{12,20},{14,22},{16,24},... | collective-permute-start | bytes 786440 | tf_op jit(solution)/shard_map/ppermute | solution.py:20
  36.3 12.6 %collective-permute-start.4 = (bf16[2,128,512]{2,1,0:T(8,128)(2,1)}, bf16[2,128,512]{2,1,0:T(8,128)(2,1)}, u32[]{:S(2)}, u32[]{:S(2)}) collective-permute-start(bf16[2,128,512]{2,1,0:T(8,128)(2,1)} %pad_maximum_fusion.9), channel_id=1, source_target_pairs={{0,6},{2,8},{4,10},{6,12},{8,14},{10,16},{12,18},{14,20},{16,22},{... | collective-permute-start | bytes 786440 | tf_op jit(solution)/shard_map/ppermute | solution.py:20
  38.7 11.2 %collective-permute-start.5 = (bf16[2,128,512]{2,1,0:T(8,128)(2,1)}, bf16[2,128,512]{2,1,0:T(8,128)(2,1)}, u32[]{:S(2)}, u32[]{:S(2)}) collective-permute-start(bf16[2,128,512]{2,1,0:T(8,128)(2,1)} %pad_maximum_fusion.9), channel_id=1, source_target_pairs={{0,4},{2,6},{4,8},{6,10},{8,12},{10,14},{12,16},{14,18},{16,20},{1... | collective-permute-start | bytes 786440 | tf_op jit(solution)/shard_map/ppermute | solution.py:20
  42.5 8.4 %collective-permute-start.6 = (bf16[2,128,512]{2,1,0:T(8,128)(2,1)}, bf16[2,128,512]{2,1,0:T(8,128)(2,1)}, u32[]{:S(2)}, u32[]{:S(2)}) collective-permute-start(bf16[2,128,512]{2,1,0:T(8,128)(2,1)} %pad_maximum_fusion.9), channel_id=1, source_target_pairs={{0,2},{2,4},{4,6},{6,8},{8,10},{10,12},{12,14},{14,16},{16,18},{18... | collective-permute-start | bytes 786440 | tf_op jit(solution)/shard_map/ppermute | solution.py:20
  59.8 10.4 %collective-permute-start.7 = (bf16[256,640]{1,0:T(8,128)(2,1)S(1)}, bf16[256,640]{1,0:T(8,128)(2,1)S(1)}, u32[]{:S(2)}, u32[]{:S(2)}) collective-permute-start(bf16[256,640]{1,0:T(8,128)(2,1)S(1)} %get-tuple-element.86), channel_id=1, source_target_pairs={{0,1},{1,0},{2,3},{3,2},{4,5},{5,4},{6,7},{7,6},{8,9},{9,8},{10,11... | collective-permute-start | bytes 983048 | tf_op jit(solution)/shard_map/ppermute | solution.py:72
  76.3 9.8 %collective-permute-start.8 = (bf16[256,640]{1,0:T(8,128)(2,1)}, bf16[256,640]{1,0:T(8,128)(2,1)}, u32[]{:S(2)}, u32[]{:S(2)}) collective-permute-start(bf16[256,640]{1,0:T(8,128)(2,1)} %get-tuple-element.90), channel_id=1, source_target_pairs={{0,1},{1,0},{2,3},{3,2},{4,5},{5,4},{6,7},{7,6},{8,9},{9,8},{10,11... | collective-permute-start | bytes 983048 | tf_op jit(solution)/shard_map/ppermute | solution.py:72
  96.1 12.8 %collective-permute-start.9 = (bf16[256,640]{1,0:T(8,128)(2,1)S(1)}, bf16[256,640]{1,0:T(8,128)(2,1)S(1)}, u32[]{:S(2)}, u32[]{:S(2)}) collective-permute-start(bf16[256,640]{1,0:T(8,128)(2,1)S(1)} %get-tuple-element.92), channel_id=1, source_target_pairs={{0,1},{1,0},{2,3},{3,2},{4,5},{5,4},{6,7},{7,6},{8,9},{9,8},{10,11... | collective-permute-start | bytes 983048 | tf_op jit(solution)/shard_map/ppermute | solution.py:72
  117.1 8.8 %collective-permute-start.14 = (bf16[2,128,512]{1,2,0:T(8,128)(2,1)S(1)}, bf16[2,128,512]{1,2,0:T(8,128)(2,1)S(1)}, u32[]{:S(2)}, u32[]{:S(2)}) collective-permute-start(bf16[2,128,512]{1,2,0:T(8,128)(2,1)S(1)} %get-tuple-element.39), channel_id=1, source_target_pairs={{8,0},{10,2},{12,4},{14,6},{16,8},{18,10},{20,12},{22,14},{24,16},... | collective-permute-start | bytes 786440 | tf_op jit(solution)/shard_map/ppermute | solution.py:20
  118.4 8.8 %collective-permute-start.13 = (bf16[2,128,512]{1,2,0:T(8,128)(2,1)S(1)}, bf16[2,128,512]{1,2,0:T(8,128)(2,1)S(1)}, u32[]{:S(2)}, u32[]{:S(2)}) collective-permute-start(bf16[2,128,512]{1,2,0:T(8,128)(2,1)S(1)} %get-tuple-element.40), channel_id=1, source_target_pairs={{6,0},{8,2},{10,4},{12,6},{14,8},{16,10},{18,12},{20,14},{22,16},{... | collective-permute-start | bytes 786440 | tf_op jit(solution)/shard_map/ppermute | solution.py:20
  119.7 13.1 %collective-permute-start.12 = (bf16[2,128,512]{1,2,0:T(8,128)(2,1)S(1)}, bf16[2,128,512]{1,2,0:T(8,128)(2,1)S(1)}, u32[]{:S(2)}, u32[]{:S(2)}) collective-permute-start(bf16[2,128,512]{1,2,0:T(8,128)(2,1)S(1)} %get-tuple-element.41), channel_id=1, source_target_pairs={{4,0},{6,2},{8,4},{10,6},{12,8},{14,10},{16,12},{18,14},{20,16},{2... | collective-permute-start | bytes 786440 | tf_op jit(solution)/shard_map/ppermute | solution.py:20
  121.0 11.8 %collective-permute-start.11 = (bf16[2,128,512]{1,2,0:T(8,128)(2,1)S(1)}, bf16[2,128,512]{1,2,0:T(8,128)(2,1)S(1)}, u32[]{:S(2)}, u32[]{:S(2)}) collective-permute-start(bf16[2,128,512]{1,2,0:T(8,128)(2,1)S(1)} %get-tuple-element.38), channel_id=1, source_target_pairs={{2,0},{4,2},{6,4},{8,6},{10,8},{12,10},{14,12},{16,14},{18,16},{20... | collective-permute-start | bytes 786440 | tf_op jit(solution)/shard_map/ppermute | solution.py:20
  133.9 7.7 %collective-permute-start.15 = (bf16[2,128,512]{1,2,0:T(8,128)(2,1)}, bf16[2,128,512]{1,2,0:T(8,128)(2,1)S(1)}, u32[]{:S(2)}, u32[]{:S(2)}) collective-permute-start(bf16[2,128,512]{1,2,0:T(8,128)(2,1)} %get-tuple-element.28), channel_id=1, source_target_pairs={{0,1},{1,0},{2,3},{3,2},{4,5},{5,4},{6,7},{7,6},{8,9},{9,8},{10,11... | collective-permute-start | bytes 786440 | tf_op jit(solution)/shard_map/ppermute | solution.py:72
  149.4 6.6 %collective-permute-start.10 = (bf16[128,640]{1,0:T(8,128)(2,1)S(1)}, bf16[128,640]{1,0:T(8,128)(2,1)S(1)}, u32[]{:S(2)}, u32[]{:S(2)}) collective-permute-start(bf16[128,640]{1,0:T(8,128)(2,1)S(1)} %slice.315), channel_id=1, source_target_pairs={{0,1},{1,0},{2,3},{3,2},{4,5},{5,4},{6,7},{7,6},{8,9},{9,8},{10,11... | collective-permute-start | bytes 491528 | tf_op jit(solution)/shard_map/ppermute | solution.py:72
  150.2 53.1 %copy-start.5 = (f32[256,640]{1,0:T(8,128)S(1)}, f32[256,640]{1,0:T(8,128)}, u32[]{:S(2)}) copy-start(f32[256,640]{1,0:T(8,128)} %copy-done.4) | copy-start | bytes 1966084
  284.2 15.1 %collective-permute-start.16 = (f32[40,512]{1,0:T(8,128)S(1)}, f32[40,512]{1,0:T(8,128)S(1)}, u32[]{:S(2)}, u32[]{:S(2)}) collective-permute-start(f32[40,512]{1,0:T(8,128)S(1)} %reshape.371), channel_id=1, source_target_pairs={{0,1},{1,0},{2,3},{3,2},{4,5},{5,4},{6,7},{7,6},{8,9},{9,8},{10,11... | collective-permute-start | bytes 245768 | tf_op jit(solution)/shard_map/ppermute | solution.py:72
  285.7 11.5 %collective-permute-start.17 = (f32[40,128]{1,0:T(8,128)S(1)}, f32[40,128]{1,0:T(8,128)S(1)}, u32[]{:S(2)}, u32[]{:S(2)}) collective-permute-start(f32[40,128]{1,0:T(8,128)S(1)} %bitcast.162), channel_id=1, source_target_pairs={{0,1},{1,0},{2,3},{3,2},{4,5},{5,4},{6,7},{7,6},{8,9},{9,8},{10,11... | collective-permute-start | bytes 61448 | tf_op jit(solution)/shard_map/ppermute | solution.py:72
  286.3 11.0 %collective-permute-start.18 = (f32[40,128]{1,0:T(8,128)S(1)}, f32[40,128]{1,0:T(8,128)S(1)}, u32[]{:S(2)}, u32[]{:S(2)}) collective-permute-start(f32[40,128]{1,0:T(8,128)S(1)} %bitcast.160), channel_id=1, source_target_pairs={{0,1},{1,0},{2,3},{3,2},{4,5},{5,4},{6,7},{7,6},{8,9},{9,8},{10,11... | collective-permute-start | bytes 61448 | tf_op jit(solution)/shard_map/ppermute | solution.py:72
  287.7 12.5 %collective-permute-start.19 = (f32[20480]{0:T(1024)S(1)}, f32[20480]{0:T(1024)S(1)}, u32[]{:S(2)}, u32[]{:S(2)}) collective-permute-start(f32[20480]{0:T(1024)S(1)} %bitcast.159), channel_id=1, source_target_pairs={{0,0},{2,1},{4,2},{6,3},{8,4},{10,5},{12,6},{14,7},{16,8},{18,9},{... | collective-permute-start | bytes 245768 | tf_op jit(solution)/shard_map/ppermute | solution.py:112
  292.1 10.4 %collective-permute-start.20 = (f32[40,1024]{1,0:T(8,128)S(1)}, f32[40,1024]{1,0:T(8,128)S(1)}, u32[]{:S(2)}, u32[]{:S(2)}) collective-permute-start(f32[40,1024]{1,0:T(8,128)S(1)} %reshape.377), channel_id=1, source_target_pairs={{0,1},{1,0},{2,3},{3,2},{4,5},{5,4},{6,7},{7,6},{8,9},{9,8},{10,11... | collective-permute-start | bytes 491528 | tf_op jit(solution)/shard_map/ppermute | solution.py:72
  297.2 9.8 %collective-permute-start.21 = (f32[40,1024]{1,0:T(8,128)S(1)}, f32[40,1024]{1,0:T(8,128)S(1)}, u32[]{:S(2)}, u32[]{:S(2)}) collective-permute-start(f32[40,1024]{1,0:T(8,128)S(1)} %reshape.378), channel_id=1, source_target_pairs={{0,1},{1,0},{2,3},{3,2},{4,5},{5,4},{6,7},{7,6},{8,9},{9,8},{10,11... | collective-permute-start | bytes 491528 | tf_op jit(solution)/shard_map/ppermute | solution.py:72
  297.3 12.0 %collective-permute-start.22 = (f32[40960]{0:T(1024)S(1)}, f32[40960]{0:T(1024)S(1)}, u32[]{:S(2)}, u32[]{:S(2)}) collective-permute-start(f32[40960]{0:T(1024)S(1)} %bitcast.158), channel_id=1, source_target_pairs={{0,0},{2,1},{4,2},{6,3},{8,4},{10,5},{12,6},{14,7},{16,8},{18,9},{... | collective-permute-start | bytes 491528 | tf_op jit(solution)/shard_map/ppermute | solution.py:112
  (69 other events, 279.9 us)
Sparse Core Ops, SparseCore 0:
  147.3 134.6 all-reduce.9

commit v2 on v1

--- a/solution.py
+++ b/solution.py
@@ -1,6 +1,8 @@
 import jax
 import jax.numpy as jnp
 from jax import lax
+from jax.experimental import pallas as pl
+from jax.experimental.pallas import tpu as pltpu
 from jax.sharding import PartitionSpec as P
 
 D = 640
@@ -111,6 +113,339 @@
         size = value.size // count
         results.append(lax.ppermute(mine[start : start + size], ("seq", "fsdp"), moves))
         start += size
+    return results
+
+
+TALL = 80
+WIDE = 1408
+DEEP = 96
+
+
+def reduce_kernel(
+    a_ref,
+    b_ref,
+    g_ref,
+    out_a,
+    out_b,
+    out_g,
+    near_a,
+    near_b,
+    sum_a,
+    sum_b,
+    side_a,
+    side_b,
+    line_a,
+    line_b,
+    far_a,
+    far_b,
+    stage_a,
+    stage_b,
+    last_a,
+    last_b,
+    gain_sent,
+    gain_got,
+    send_near,
+    recv_near,
+    send_side,
+    recv_side,
+    send_far,
+    recv_far,
+    send_last,
+    recv_last,
+    send_gain,
+    recv_gain,
+):
+    s = lax.axis_index("seq")
+    f = lax.axis_index("fsdp")
+    core = lax.rem(s, 2)
+    chip = s // 2
+    x = lax.rem(chip, 2)
+    z = chip // 2
+    mesh_id = pl.DeviceIdType.MESH
+    sibling = (chip * 2 + 1 - core, f)
+    beside = ((z * 2 + 1 - x) * 2 + core, f)
+    across = (s, 1 - f)
+    diagonal = (chip * 2 + 1 - core, 1 - f)
+    along = [((lax.rem(z + d, 4) * 2 + x) * 2 + core, f) for d in range(4)]
+    targets = [(8 * f + chip, k) for k in range(2)]
+    sources = [(2 * lax.rem(s, 8) + c, s // 8) for c in range(2)]
+
+    def elsewhere(place):
+        return jnp.logical_or(place[0] != s, place[1] != f)
+
+    barrier = pltpu.get_barrier_semaphore()
+    greeted = [sibling, beside, across, diagonal] + along[1:]
+    for place in greeted:
+        pl.semaphore_signal(barrier, inc=1, device_id=place, device_id_type=mesh_id)
+    others = jnp.int32(len(greeted))
+    for place in targets + sources:
+        others = others + elsewhere(place).astype(jnp.int32)
+
+        @pl.when(elsewhere(place))
+        def _():
+            pl.semaphore_signal(barrier, inc=1, device_id=place, device_id_type=mesh_id)
+
+    pl.semaphore_wait(barrier, others)
+
+    def remote(source, target, sent, got, place):
+        return pltpu.make_async_remote_copy(
+            src_ref=source,
+            dst_ref=target,
+            send_sem=sent,
+            recv_sem=got,
+            device_id=place,
+            device_id_type=mesh_id,
+        )
+
+    def part_a(unit, half):
+        return a_ref.at[unit, :, pl.ds(pl.multiple_of(half * WIDE, 128), WIDE)]
+
+    lines = [lax.rem(z + d, 4) for d in (2, 1, 3, 0)]
+
+    def gain_copy(step, slot, place):
+        return remote(
+            gain_sent.at[step], gain_got.at[slot], send_gain.at[slot], recv_gain.at[slot], place
+        )
+
+    gain_sent[0] = g_ref[...]
+    gain_near = gain_copy(0, 0, sibling)
+    gain_near.start()
+    near = []
+    for xh in (1 - x, x):
+        for zh in lines:
+            unit = zh * 2 + xh
+            near.append(
+                (
+                    remote(
+                        part_a(unit, 1 - core),
+                        near_a.at[unit],
+                        send_near.at[0, unit],
+                        recv_near.at[0, unit],
+                        sibling,
+                    ),
+                    remote(
+                        b_ref.at[unit, 1 - core],
+                        near_b.at[unit],
+                        send_near.at[1, unit],
+                        recv_near.at[1, unit],
+                        sibling,
+                    ),
+                )
+            )
+            for copy in near[-1]:
+                copy.start()
+    gain_near.wait()
+    gain_sent[1] = gain_sent[0] + gain_got[0]
+    gain_side = gain_copy(1, 1, beside)
+    gain_side.start()
+    side = []
+    for step in range(4):
+        zh = lines[step]
+        unit = zh * 2 + 1 - x
+        for copy in near[step]:
+            copy.wait_recv()
+        sum_a[step] = (
+            part_a(unit, core)[...].astype(jnp.float32) + near_a[unit].astype(jnp.float32)
+        ).astype(jnp.bfloat16)
+        sum_b[step] = (
+            b_ref[unit, core].astype(jnp.float32) + near_b[unit].astype(jnp.float32)
+        ).astype(jnp.bfloat16)
+        side.append(
+            (
+                remote(
+                    sum_a.at[step],
+                    side_a.at[step],
+                    send_side.at[0, step],
+                    recv_side.at[0, step],
+                    beside,
+                ),
+                remote(
+                    sum_b.at[step],
+                    side_b.at[step],
+                    send_side.at[1, step],
+                    recv_side.at[1, step],
+                    beside,
+                ),
+            )
+        )
+        for copy in side[-1]:
+            copy.start()
+    gain_side.wait()
+    gain_sent[2] = gain_sent[1] + gain_got[1]
+    gain_line = [gain_copy(2, 1 + d, along[d]) for d in (1, 2, 3)]
+    for copy in gain_line:
+        copy.start()
+    far = []
+    for step in range(4):
+        unit = lines[step] * 2 + x
+        for copy in near[4 + step]:
+            copy.wait_recv()
+        for copy in side[step]:
+            copy.wait_recv()
+        total_a = (
+            part_a(unit, core)[...].astype(jnp.float32)
+            + near_a[unit].astype(jnp.float32)
+            + side_a[step].astype(jnp.float32)
+        )
+        total_b = (
+            b_ref[unit, core].astype(jnp.float32)
+            + near_b[unit].astype(jnp.float32)
+            + side_b[step].astype(jnp.float32)
+        )
+        if step < 3:
+            distance = (2, 1, 3)[step]
+            line_a[step] = total_a.astype(jnp.bfloat16)
+            line_b[step] = total_b.astype(jnp.bfloat16)
+            far.append(
+                (
+                    remote(
+                        line_a.at[step],
+                        far_a.at[step],
+                        send_far.at[0, step],
+                        recv_far.at[0, step],
+                        along[distance],
+                    ),
+                    remote(
+                        line_b.at[step],
+                        far_b.at[step],
+                        send_far.at[1, step],
+                        recv_far.at[1, step],
+                        along[distance],
+                    ),
+                )
+            )
+            for copy in far[-1]:
+                copy.start()
+    for copy in gain_line:
+        copy.wait()
+    gain_sent[3] = (gain_sent[2] + gain_got[2]) + (gain_got[3] + gain_got[4])
+    gain_cross = gain_copy(3, 5, across)
+    gain_cross.start()
+    for pair in far:
+        for copy in pair:
+            copy.wait_recv()
+    total_a = total_a + far_a[0].astype(jnp.float32)
+    total_a = total_a + far_a[1].astype(jnp.float32) + far_a[2].astype(jnp.float32)
+    for k in range(4):
+        stage_a[k, 0:20, :] = total_a[20 * k : 20 * k + 20]
+        stage_a[k, 20:24, :] = jnp.zeros((4, WIDE), jnp.float32)
+    total_b = total_b + far_b[0].astype(jnp.float32)
+    total_b = total_b + far_b[1].astype(jnp.float32) + far_b[2].astype(jnp.float32)
+    for k in range(2):
+        stage_b[k] = total_b[48 * k : 48 * k + 48]
+    me = 2 * core + f
+    last = []
+    for step, place in enumerate((across, diagonal, sibling)):
+        goal = 2 * lax.rem(place[0], 2) + place[1]
+        copy = remote(
+            stage_a.at[goal], last_a.at[me], send_last.at[0, step], recv_last.at[0, step], place
+        )
+        copy.start()
+        last.append(copy)
+    moves = [
+        remote(
+            stage_b.at[k], last_b.at[core], send_last.at[1, k], recv_last.at[1, core], targets[k]
+        )
+        for k in range(2)
+    ]
+    for k in range(2):
+        pl.when(elsewhere(targets[k]))(moves[k].start)
+
+        @pl.when(jnp.logical_not(elsewhere(targets[k])))
+        def _():
+            last_b[core] = stage_b[k]
+
+    last_a[me] = stage_a[me]
+    gain_cross.wait()
+    out_g[...] = gain_sent[3] + gain_got[5]
+    for copy in last:
+        copy.wait_recv()
+    out_a[...] = last_a[...]
+    for c in range(2):
+        arrival = remote(
+            stage_b.at[0], last_b.at[c], send_last.at[1, 0], recv_last.at[1, c], sibling
+        )
+        pl.when(elsewhere(sources[c]))(arrival.wait_recv)
+    out_b[...] = last_b[...]
+    for pair in near + side + far:
+        for copy in pair:
+            copy.wait_send()
+    for copy in last:
+        copy.wait_send()
+    for k in range(2):
+        pl.when(elsewhere(targets[k]))(moves[k].wait_send)
+
+
+def reduce_planes(columns, rows, grad_gains, fsdp):
+    low = jnp.bfloat16
+    a = jnp.concatenate([value.astype(low) for value in columns], axis=1)
+    a = a.reshape(8, TALL, 2 * WIDE)
+    b = jnp.concatenate(
+        [value.astype(low).reshape(8, 2, 2, -1, D).transpose(0, 2, 1, 3, 4) for value in rows],
+        axis=3,
+    ).reshape(8, 2, DEEP, D)
+    f32 = jnp.float32
+    vmem = pl.BlockSpec(memory_space=pltpu.VMEM)
+    dma = pltpu.SemaphoreType.DMA
+    last_a, last_b, gain_sum = pl.pallas_call(
+        reduce_kernel,
+        out_shape=(
+            jax.ShapeDtypeStruct((4, 24, WIDE), f32),
+            jax.ShapeDtypeStruct((2, DEEP // 2, D), f32),
+            jax.ShapeDtypeStruct((24, 128), f32),
+        ),
+        in_specs=[vmem] * 3,
+        out_specs=(vmem,) * 3,
+        scratch_shapes=[
+            pltpu.VMEM((8, TALL, WIDE), low),
+            pltpu.VMEM((8, DEEP, D), low),
+            pltpu.VMEM((4, TALL, WIDE), low),
+            pltpu.VMEM((4, DEEP, D), low),
+            pltpu.VMEM((4, TALL, WIDE), low),
+            pltpu.VMEM((4, DEEP, D), low),
+            pltpu.VMEM((3, TALL, WIDE), low),
+            pltpu.VMEM((3, DEEP, D), low),
+            pltpu.VMEM((3, TALL, WIDE), low),
+            pltpu.VMEM((3, DEEP, D), low),
+            pltpu.VMEM((4, 24, WIDE), f32),
+            pltpu.VMEM((2, DEEP // 2, D), f32),
+            pltpu.VMEM((4, 24, WIDE), f32),
+            pltpu.VMEM((2, DEEP // 2, D), f32),
+            pltpu.VMEM((4, 24, 128), f32),
+            pltpu.VMEM((6, 24, 128), f32),
+            dma((2, 8)),
+            dma((2, 8)),
+            dma((2, 4)),
+            dma((2, 4)),
+            dma((2, 3)),
+            dma((2, 3)),
+            dma((2, 3)),
+            dma((2, 3)),
+            dma((6,)),
+            dma((6,)),
+        ],
+        compiler_params=pltpu.CompilerParams(
+            collective_id=0, has_side_effects=True, vmem_limit_bytes=40 * 1024 * 1024
+        ),
+    )(a, b, grad_gains.reshape(24, 128))
+    piece = last_a[:, :20].reshape(2, 2, 20, WIDE)
+    halves = [jnp.concatenate([piece[0, plane], piece[1, plane]], axis=1) for plane in range(2)]
+    results = []
+    start = 0
+    for value in columns:
+        stop = start + value.shape[1]
+        results.append(
+            jnp.concatenate([half[:, start:stop] for half in halves], axis=1).reshape(-1)
+        )
+        start = stop
+    start = 0
+    for value in rows:
+        stop = start + value.shape[0] // 32
+        results.append(last_b[:, start:stop].reshape(-1))
+        start = stop
+    place = lax.axis_index("seq") * 2 + fsdp
+    size = grad_gains.shape[0] // 32
+    results.append(lax.dynamic_slice_in_dim(gain_sum.reshape(-1), place * size, size))
     return results
 
 
@@ -266,11 +601,16 @@
             0.5 * d_gain_key,
         ]
     )
-    flat_gate, flat_up, flat_down = reduce_generic([grad_gate, grad_up], [grad_down], fsdp)
-    flat_q, flat_k, flat_v, flat_o = reduce_generic([grad_q, grad_k, grad_v], [grad_o], fsdp)
-    flat_gains = lax.psum_scatter(
-        grad_gains, ("seq", "fsdp"), scatter_dimension=0, tiled=True
-    )
+    columns = [grad_q, grad_k, grad_v, grad_gate, grad_up]
+    if lax.axis_size("seq") == 16:
+        reduced = reduce_planes(columns, [grad_down, grad_o], grad_gains, fsdp)
+        flat_q, flat_k, flat_v, flat_gate, flat_up, flat_down, flat_o, flat_gains = reduced
+    else:
+        reduced = reduce_generic(columns, [grad_down, grad_o], fsdp)
+        flat_q, flat_k, flat_v, flat_gate, flat_up, flat_down, flat_o = reduced
+        flat_gains = lax.psum_scatter(
+            grad_gains, ("seq", "fsdp"), scatter_dimension=0, tiled=True
+        )
     return (
         output_b[None],
         d_tokens[None],

time: 319 us -> 239 us (0.75)
  waiting for transfers between devices: 129 us -> 53.1 us
  Pallas kernels: 0 us -> 62.1 us
  blocking collectives: 45.4 us -> 0 us
  between operations: 15.4 us -> 1.89 us
  starting transfers between devices: 40.2 us -> 27.3 us
  matrix products: 25.7 us -> 32.9 us
    unnamed x2 -> x0, waiting for transfers between devices: 77.8 us -> none
    pallas_call x0 -> x1, Pallas kernels: none -> 62.1 us  [reduce_planes(): pl.pallas_call(reduce_kernel, out_shape=(jax.ShapeDtypeStruct((4, 24, WID...]
    unnamed x1 -> x0, blocking collectives: 45.4 us -> none
    ppermute x13 -> x8, starting transfers between devices: 19.7 us -> 8.15 us  [swapped(): return lax.ppermute(value, 'fsdp', [(0, 1), (1, 0)])]
    ppermute x8, waiting for transfers between devices: 9.1 us -> 17 us  [shifted(): lax.ppermute(value, axis, [(source, source + steps) for source in range(l...]
    ppermute x13 -> x8, waiting for transfers between devices: 42.1 us -> 36.1 us  [swapped(): return lax.ppermute(value, 'fsdp', [(0, 1), (1, 0)])]
    convert_element_type x0 -> x3, local copies, waits for them, and re-layouts: none -> 4.95 us  [reduce_planes(): a = jnp.concatenate([value.astype(low) for value in columns], axis=1)]
    convert_element_type x2 -> x0, other arithmetic: 4.53 us -> none  [reduce_generic(): mine = mine.astype(jnp.float32).reshape(-1)]
  transfers between devices with their start and end apart: 24 -> 16, of which waited for: 11 -> 9; matrix products, arithmetic and copies ran while one was open for 12% -> 18% of each run, Pallas kernels for 0% -> 0%
where the time goes in v2:
time: 239 us; the launch traced here: 238 us
  Pallas kernels  62.1 us (26%)
  waiting for transfers between devices  53.1 us (22%)
  local copies, waits for them, and re-layouts  38.7 us (16%)
  matrix products  32.9 us (14%)
  starting transfers between devices  27.3 us (11%)
  other arithmetic  21.9 us (9%)
    pallas_call x1, Pallas kernels, reduce_planes(): pl.pallas_call(reduce_kernel, out_shape=(jax.ShapeDtypeStruct((4, 24, WID...  62.1 us
    ppermute x8, waiting for transfers between devices, swapped(): return lax.ppermute(value, 'fsdp', [(0, 1), (1, 0)])  36.1 us
    ppermute x8, starting transfers between devices, shifted(): lax.ppermute(value, axis, [(source, source + steps) for source in range(l...  19.2 us
    ppermute x8, waiting for transfers between devices, shifted(): lax.ppermute(value, axis, [(source, source + steps) for source in range(l...  17 us
    unnamed x156, local copies, waits for them, and re-layouts  16.1 us
    dot_general x7, matrix products, inner_left(): lax.dot_general(left_side, right_side, (((0,), (0,)), ((), ())), preferre...  9.68 us
    ppermute x8, starting transfers between devices, swapped(): return lax.ppermute(value, 'fsdp', [(0, 1), (1, 0)])  8.15 us
    dot_general x7, matrix products, inner_right(): lax.dot_general(left_side, right_side, (((1,), (1,)), ((), ())), preferre...  7.44 us
  transfers between devices with their start and end apart: 16, of which 9 were waited for; matrix products, arithmetic and copies ran while one was open for 18% of the time, Pallas kernels for 0%

profile of v2, /device:TPU:0, one launch (start us, length us, event | category | flops | bytes accessed | tf_op | source)
XLA Modules:
  0.0 238.0 jit_solution(5362323881556478869)
XLA Ops:
  0.7 3.0 %collective-permute-start.2 = (s32[1,128]{1,0:T(1,128)}, s32[1,128]{1,0:T(1,128)S(1)}, u32[]{:S(2)}, u32[]{:S(2)}) collective-permute-start(s32[1,128]{1,0:T(1,128)} %param.20), channel_id=1, source_target_pairs={{0,1},{1,0},{2,3},{3,2},{4,5},{5,4},{6,7},{7,6},{8,9},{9,8},{10,11... | collective-permute-start | bytes 1544 | tf_op jit(solution)/shard_map/ppermute | solution.py:74
  4.9 1.7 pad_maximum_fusion.2
  6.7 1.9 collective-permute-start
  9.6 11.4 %collective-permute-done = bf16[256,640]{1,0:T(8,128)(2,1)S(1)} collective-permute-done((bf16[256,640]{1,0:T(8,128)(2,1)}, bf16[256,640]{1,0:T(8,128)(2,1)S(1)}, u32[]{:S(2)}, u32[]{:S(2)}) %collective-permute-start) | collective-permute-done | bytes 327712 | tf_op jit(solution)/shard_map/ppermute | solution.py:74
  24.9 2.0 collective-permute-start.6
  26.9 4.0 %collective-permute-start.5 = (bf16[2,128,512]{2,1,0:T(8,128)(2,1)}, bf16[2,128,512]{2,1,0:T(8,128)(2,1)}, u32[]{:S(2)}, u32[]{:S(2)}) collective-permute-start(bf16[2,128,512]{2,1,0:T(8,128)(2,1)} %pad_maximum_fusion.8), channel_id=1, source_target_pairs={{0,4},{2,6},{4,8},{6,10},{8,12},{10,14},{12,16},{14,18},{16,20},{1... | collective-permute-start | bytes 786440 | tf_op jit(solution)/shard_map/ppermute | solution.py:22
  30.9 4.4 %collective-permute-start.4 = (bf16[2,128,512]{2,1,0:T(8,128)(2,1)}, bf16[2,128,512]{2,1,0:T(8,128)(2,1)}, u32[]{:S(2)}, u32[]{:S(2)}) collective-permute-start(bf16[2,128,512]{2,1,0:T(8,128)(2,1)} %pad_maximum_fusion.8), channel_id=1, source_target_pairs={{0,6},{2,8},{4,10},{6,12},{8,14},{10,16},{12,18},{14,20},{16,22},{... | collective-permute-start | bytes 786440 | tf_op jit(solution)/shard_map/ppermute | solution.py:22
  35.3 3.5 %collective-permute-start.3 = (bf16[2,128,512]{2,1,0:T(8,128)(2,1)}, bf16[2,128,512]{2,1,0:T(8,128)(2,1)}, u32[]{:S(2)}, u32[]{:S(2)}) collective-permute-start(bf16[2,128,512]{2,1,0:T(8,128)(2,1)} %pad_maximum_fusion.8), channel_id=1, source_target_pairs={{0,8},{2,10},{4,12},{6,14},{8,16},{10,18},{12,20},{14,22},{16,24},... | collective-permute-start | bytes 786440 | tf_op jit(solution)/shard_map/ppermute | solution.py:22
  41.3 2.1 collective-permute-done.3
  45.0 1.7 constant_dynamic-update-slice_fusion.3
  50.8 2.8 %fusion.108 = (f32[2,2,128]{2,1,0:T(2,128)S(1)}, f32[2,2,128,640]{2,3,1,0:T(8,128)}) fusion(pred[2,128,640]{1,2,0:T(8,128)(4,1)S(1)} %copy-done.58, bf16[2,640,512]{2,1,0:T(8,128)(2,1)} %constant_dynamic-update-slice_fusion, bf16[2,128,2,128]{3,1,0,2:T(8,128)(2,1)S(1)} %bitcast.173, bf16[2,128,2,128]{3,1,0,2:T(8,128)(2,1)S(1)} %bitcast.171), kind=kOutput, calls=%fused_computation.233 | convolution fusion | flops 169607808 | bytes 2394112 | tf_op jit(solution)/shard_map/sub | solution.py:516
  53.6 1.9 fusion.10
  56.5 2.2 fusion.111
  59.3 7.5 %collective-permute-done.7 = bf16[256,640]{1,0:T(8,128)(2,1)S(1)} collective-permute-done((bf16[256,640]{1,0:T(8,128)(2,1)}, bf16[256,640]{1,0:T(8,128)(2,1)S(1)}, u32[]{:S(2)}, u32[]{:S(2)}) %collective-permute-start.7) | collective-permute-done | bytes 327712 | tf_op jit(solution)/shard_map/ppermute | solution.py:74
  72.4 5.9 %collective-permute-done.8 = bf16[256,640]{1,0:T(8,128)(2,1)S(1)} collective-permute-done((bf16[256,640]{1,0:T(8,128)(2,1)S(1)}, bf16[256,640]{1,0:T(8,128)(2,1)S(1)}, u32[]{:S(2)}, u32[]{:S(2)}) %collective-permute-start.8) | collective-permute-done | bytes 327712 | tf_op jit(solution)/shard_map/ppermute | solution.py:74
  84.6 3.9 %collective-permute-done.9 = bf16[256,640]{1,0:T(8,128)(2,1)S(1)} collective-permute-done((bf16[256,640]{1,0:T(8,128)(2,1)S(1)}, bf16[256,640]{1,0:T(8,128)(2,1)S(1)}, u32[]{:S(2)}, u32[]{:S(2)}) %collective-permute-start.9) | collective-permute-done | bytes 327712 | tf_op jit(solution)/shard_map/ppermute | solution.py:74
  91.7 1.7 reshape.331
  93.5 1.8 copy.144
  95.3 2.5 %convolution_bitcast_fusion = f32[2,640,256]{1,2,0:T(8,128)} fusion(bf16[2,128,2,256]{1,3,2,0:T(8,128)(2,1)} %copy.144, f32[2,2,128,640]{2,3,1,0:T(8,128)S(1)} %copy-done.24, f32[2,2,128]{2,1,0:T(2,128)S(1)} %copy-done.64), kind=kOutput, calls=%fused_computation.18 | convolution fusion | flops 168427520 | bytes 2885632 | tf_op jit(solution)/shard_map/bhtk,bthd->bkd/dot_general | solution.py:560
  117.1 2.2 copy.146
  119.2 9.3 %collective-permute-done.14 = bf16[2,128,512]{1,2,0:T(8,128)(2,1)} collective-permute-done((bf16[2,128,512]{1,2,0:T(8,128)(2,1)}, bf16[2,128,512]{1,2,0:T(8,128)(2,1)}, u32[]{:S(2)}, u32[]{:S(2)}) %collective-permute-start.14) | collective-permute-done | bytes 262176 | tf_op jit(solution)/shard_map/ppermute | solution.py:22
  128.6 2.1 collective-permute-done.13
  130.7 3.5 %collective-permute-done.12 = bf16[2,128,512]{1,2,0:T(8,128)(2,1)} collective-permute-done((bf16[2,128,512]{1,2,0:T(8,128)(2,1)}, bf16[2,128,512]{1,2,0:T(8,128)(2,1)}, u32[]{:S(2)}, u32[]{:S(2)}) %collective-permute-start.12) | collective-permute-done | bytes 262176 | tf_op jit(solution)/shard_map/ppermute | solution.py:22
  137.4 7.4 %collective-permute-done.15 = bf16[2,128,512]{1,2,0:T(8,128)(2,1)S(1)} collective-permute-done((bf16[2,128,512]{1,2,0:T(8,128)(2,1)S(1)}, bf16[2,128,512]{1,2,0:T(8,128)(2,1)S(1)}, u32[]{:S(2)}, u32[]{:S(2)}) %collective-permute-start.15) | collective-permute-done | bytes 262176 | tf_op jit(solution)/shard_map/ppermute | solution.py:74
  145.7 2.1 copy.145
  147.8 1.8 bitcast_convert_fusion
  153.2 1.7 copy.147
  155.8 1.9 convolution_convert_fusion.7
  161.1 2.8 %fusion.2 = bf16[640,2816]{1,0:T(8,128)(2,1)} fusion(bf16[640,2816]{1,0:T(8,128)(2,1)} %constant_dynamic-update-slice_fusion.5, bf16[256,640]{1,0:T(8,128)(2,1)} %copy-done.26, bf16[256,1024]{1,0:T(8,128)(2,1)} %copy-done.40), kind=kOutput, calls=%fused_computation.9 | convolution fusion | flops 336199680 | bytes 2162688 | tf_op jit(solution)/shard_map/dot_general | solution.py:62
  166.0 2.1 multiply_reduce_fusion.11
  168.2 62.1 %shard_map.186 = (f32[4,24,1408]{2,1,0:T(8,128)S(1)}, f32[2,48,640]{2,1,0:T(8,128)S(1)}, f32[24,128]{1,0:T(8,128)S(1)}) custom-call(bf16[8,80,2816]{2,1,0:T(8,128)(2,1)S(1)} %bitcast.135, bf16[8,2,96,640]{3,2,1,0:T(8,128)(2,1)S(1)} %bitcast.134, f32[24,128]{1,0:T(8,128)S(1)} %bitcast.137), custom_call_target="tpu_custom_call" | custom-call | tf_op jit(solution)/shard_map/pallas_call | solution.py:390
  235.5 1.8 fusion.35
  (286 shorter events, 69.2 us)
Async XLA Ops:
  0.6 69.8 %copy-start = (bf16[1024,640]{1,0:T(8,128)(2,1)S(1)}, bf16[1024,640]{1,0:T(8,128)(2,1)}, u32[]{:S(2)}) copy-start(bf16[1024,640]{1,0:T(8,128)(2,1)} %param.18) | copy-start | bytes 3932164
  0.7 8.1 %collective-permute-start.2 = (s32[1,128]{1,0:T(1,128)}, s32[1,128]{1,0:T(1,128)S(1)}, u32[]{:S(2)}, u32[]{:S(2)}) collective-permute-start(s32[1,128]{1,0:T(1,128)} %param.20), channel_id=1, source_target_pairs={{0,1},{1,0},{2,3},{3,2},{4,5},{5,4},{6,7},{7,6},{8,9},{9,8},{10,11... | collective-permute-start | bytes 1544 | tf_op jit(solution)/shard_map/ppermute | solution.py:74
  4.7 16.3 %copy-start.9 = (bf16[1,128,640]{2,1,0:T(8,128)(2,1)S(1)}, bf16[1,128,640]{2,1,0:T(8,128)(2,1)}, u32[]{:S(2)}) copy-start(bf16[1,128,640]{2,1,0:T(8,128)(2,1)} %param.11) | copy-start | bytes 491524
  4.8 16.5 %collective-permute-start.1 = (bf16[640,256]{1,0:T(8,128)(2,1)S(1)}, bf16[640,256]{1,0:T(8,128)(2,1)S(1)}, u32[]{:S(2)}, u32[]{:S(2)}) collective-permute-start(bf16[640,256]{1,0:T(8,128)(2,1)S(1)} %pad_maximum_fusion.5), channel_id=1, source_target_pairs={{0,1},{1,0},{2,3},{3,2},{4,5},{5,4},{6,7},{7,6},{8,9},{9,8},{10,11... | collective-permute-start | bytes 983048 | tf_op jit(solution)/shard_map/ppermute | solution.py:74
  6.7 14.3 %collective-permute-start = (bf16[256,640]{1,0:T(8,128)(2,1)}, bf16[256,640]{1,0:T(8,128)(2,1)S(1)}, u32[]{:S(2)}, u32[]{:S(2)}) collective-permute-start(bf16[256,640]{1,0:T(8,128)(2,1)} %pad_maximum_fusion.2), channel_id=1, source_target_pairs={{0,1},{1,0},{2,3},{3,2},{4,5},{5,4},{6,7},{7,6},{8,9},{9,8},{10,11... | collective-permute-start | bytes 983048 | tf_op jit(solution)/shard_map/ppermute | solution.py:74
  8.6 12.7 %copy-start.52 = (bf16[640,128]{1,0:T(8,128)(2,1)S(1)}, bf16[640,128]{1,0:T(8,128)(2,1)}, u32[]{:S(2)}) copy-start(bf16[640,128]{1,0:T(8,128)(2,1)} %param.14) | copy-start | bytes 491524
  8.7 14.2 %copy-start.65 = (f32[128]{0:T(128)}, f32[128]{0:T(128)S(1)}, u32[]{:S(2)}) copy-start(f32[128]{0:T(128)S(1)} %multiply_power_fusion) | copy-start | bytes 1540
  21.0 46.0 %copy-start.12 = (bf16[128,640]{1,0:T(8,128)(2,1)}, bf16[128,640]{1,0:T(8,128)(2,1)S(1)}, u32[]{:S(2)}) copy-start(bf16[128,640]{1,0:T(8,128)(2,1)S(1)} %get-tuple-element.63) | copy-start | bytes 491524
  21.2 17.6 %copy-start.67 = (f32[256]{0:T(256)}, f32[256]{0:T(256)S(1)}, u32[]{:S(2)}) copy-start(f32[256]{0:T(256)S(1)} %add_rsqrt_fusion) | copy-start | bytes 3076
  22.8 16.5 %copy-start.20 = (f32[256,256]{1,0:T(8,128)}, f32[256,256]{1,0:T(8,128)S(1)}, u32[]{:S(2)}) copy-start(f32[256,256]{1,0:T(8,128)S(1)} %get-tuple-element.88) | copy-start | bytes 786436
  22.8 16.1 %copy-start.35 = (bf16[640,512]{1,0:T(8,128)(2,1)S(1)}, bf16[640,512]{1,0:T(8,128)(2,1)}, u32[]{:S(2)}) copy-start(bf16[640,512]{1,0:T(8,128)(2,1)} %param.12) | copy-start | bytes 1966084
  24.1 14.7 %copy-start.36 = (bf16[256,128]{1,0:T(8,128)(2,1)}, bf16[256,128]{1,0:T(8,128)(2,1)S(1)}, u32[]{:S(2)}) copy-start(bf16[256,128]{1,0:T(8,128)(2,1)S(1)} %get-tuple-element.81) | copy-start | bytes 196612
  24.1 14.7 %copy-start.38 = (bf16[256,128]{1,0:T(8,128)(2,1)}, bf16[256,128]{1,0:T(8,128)(2,1)S(1)}, u32[]{:S(2)}) copy-start(bf16[256,128]{1,0:T(8,128)(2,1)S(1)} %get-tuple-element.82) | copy-start | bytes 196612
  24.1 16.1 %copy-start.28 = (f32[256,128]{1,0:T(8,128)}, f32[256,128]{1,0:T(8,128)S(1)}, u32[]{:S(2)}) copy-start(f32[256,128]{1,0:T(8,128)S(1)} %get-tuple-element.79) | copy-start | bytes 393220
  24.9 23.5 %collective-permute-start.6 = (bf16[2,128,512]{2,1,0:T(8,128)(2,1)}, bf16[2,128,512]{2,1,0:T(8,128)(2,1)}, u32[]{:S(2)}, u32[]{:S(2)}) collective-permute-start(bf16[2,128,512]{2,1,0:T(8,128)(2,1)} %pad_maximum_fusion.8), channel_id=1, source_target_pairs={{0,2},{2,4},{4,6},{6,8},{8,10},{10,12},{12,14},{14,16},{16,18},{18... | collective-permute-start | bytes 786440 | tf_op jit(solution)/shard_map/ppermute | solution.py:22
  26.9 19.8 %collective-permute-start.5 = (bf16[2,128,512]{2,1,0:T(8,128)(2,1)}, bf16[2,128,512]{2,1,0:T(8,128)(2,1)}, u32[]{:S(2)}, u32[]{:S(2)}) collective-permute-start(bf16[2,128,512]{2,1,0:T(8,128)(2,1)} %pad_maximum_fusion.8), channel_id=1, source_target_pairs={{0,4},{2,6},{4,8},{6,10},{8,12},{10,14},{12,16},{14,18},{16,20},{1... | collective-permute-start | bytes 786440 | tf_op jit(solution)/shard_map/ppermute | solution.py:22
  30.9 14.1 %collective-permute-start.4 = (bf16[2,128,512]{2,1,0:T(8,128)(2,1)}, bf16[2,128,512]{2,1,0:T(8,128)(2,1)}, u32[]{:S(2)}, u32[]{:S(2)}) collective-permute-start(bf16[2,128,512]{2,1,0:T(8,128)(2,1)} %pad_maximum_fusion.8), channel_id=1, source_target_pairs={{0,6},{2,8},{4,10},{6,12},{8,14},{10,16},{12,18},{14,20},{16,22},{... | collective-permute-start | bytes 786440 | tf_op jit(solution)/shard_map/ppermute | solution.py:22
  35.3 8.1 %collective-permute-start.3 = (bf16[2,128,512]{2,1,0:T(8,128)(2,1)}, bf16[2,128,512]{2,1,0:T(8,128)(2,1)}, u32[]{:S(2)}, u32[]{:S(2)}) collective-permute-start(bf16[2,128,512]{2,1,0:T(8,128)(2,1)} %pad_maximum_fusion.8), channel_id=1, source_target_pairs={{0,8},{2,10},{4,12},{6,14},{8,16},{10,18},{12,20},{14,22},{16,24},... | collective-permute-start | bytes 786440 | tf_op jit(solution)/shard_map/ppermute | solution.py:22
  41.2 9.6 %copy-start.43 = (bf16[256,2,128]{2,0,1:T(8,128)(2,1)}, bf16[256,2,128]{2,0,1:T(8,128)(2,1)S(1)}, u32[]{:S(2)}) copy-start(bf16[256,2,128]{2,0,1:T(8,128)(2,1)S(1)} %get-tuple-element.47) | copy-start | bytes 393220
  41.2 9.6 %copy-start.45 = (bf16[256,2,128]{2,0,1:T(8,128)(2,1)}, bf16[256,2,128]{2,0,1:T(8,128)(2,1)S(1)}, u32[]{:S(2)}) copy-start(bf16[256,2,128]{2,0,1:T(8,128)(2,1)S(1)} %get-tuple-element.48) | copy-start | bytes 393220
  41.3 9.6 %copy-start.58 = (pred[2,128,640]{1,2,0:T(8,128)(4,1)S(1)}, pred[2,128,640]{1,2,0:T(8,128)(4,1)}, u32[]{:S(2)}) copy-start(pred[2,128,640]{1,2,0:T(8,128)(4,1)} %and_and_fusion) | copy-start | bytes 491524
  58.7 8.1 %collective-permute-start.7 = (bf16[256,640]{1,0:T(8,128)(2,1)}, bf16[256,640]{1,0:T(8,128)(2,1)S(1)}, u32[]{:S(2)}, u32[]{:S(2)}) collective-permute-start(bf16[256,640]{1,0:T(8,128)(2,1)} %get-tuple-element.91), channel_id=1, source_target_pairs={{0,1},{1,0},{2,3},{3,2},{4,5},{5,4},{6,7},{7,6},{8,9},{9,8},{10,11... | collective-permute-start | bytes 983048 | tf_op jit(solution)/shard_map/ppermute | solution.py:74
  59.3 12.4 %copy-start.16 = (f32[256,640]{1,0:T(8,128)}, f32[256,640]{1,0:T(8,128)S(1)}, u32[]{:S(2)}) copy-start(f32[256,640]{1,0:T(8,128)S(1)} %fusion.93) | copy-start | bytes 1966084
  71.1 7.1 %collective-permute-start.8 = (bf16[256,640]{1,0:T(8,128)(2,1)S(1)}, bf16[256,640]{1,0:T(8,128)(2,1)S(1)}, u32[]{:S(2)}, u32[]{:S(2)}) collective-permute-start(bf16[256,640]{1,0:T(8,128)(2,1)S(1)} %get-tuple-element.95), channel_id=1, source_target_pairs={{0,1},{1,0},{2,3},{3,2},{4,5},{5,4},{6,7},{7,6},{8,9},{9,8},{10,11... | collective-permute-start | bytes 983048 | tf_op jit(solution)/shard_map/ppermute | solution.py:74
  81.4 7.1 %collective-permute-start.9 = (bf16[256,640]{1,0:T(8,128)(2,1)S(1)}, bf16[256,640]{1,0:T(8,128)(2,1)S(1)}, u32[]{:S(2)}, u32[]{:S(2)}) collective-permute-start(bf16[256,640]{1,0:T(8,128)(2,1)S(1)} %get-tuple-element.97), channel_id=1, source_target_pairs={{0,1},{1,0},{2,3},{3,2},{4,5},{5,4},{6,7},{7,6},{8,9},{9,8},{10,11... | collective-permute-start | bytes 983048 | tf_op jit(solution)/shard_map/ppermute | solution.py:74
  107.8 11.5 %collective-permute-start.11 = (bf16[2,128,512]{1,2,0:T(8,128)(2,1)}, bf16[2,128,512]{1,2,0:T(8,128)(2,1)}, u32[]{:S(2)}, u32[]{:S(2)}) collective-permute-start(bf16[2,128,512]{1,2,0:T(8,128)(2,1)} %get-tuple-element.40), channel_id=1, source_target_pairs={{2,0},{4,2},{6,4},{8,6},{10,8},{12,10},{14,12},{16,14},{18,16},{20... | collective-permute-start | bytes 786440 | tf_op jit(solution)/shard_map/ppermute | solution.py:22
  109.0 19.5 %collective-permute-start.14 = (bf16[2,128,512]{1,2,0:T(8,128)(2,1)}, bf16[2,128,512]{1,2,0:T(8,128)(2,1)}, u32[]{:S(2)}, u32[]{:S(2)}) collective-permute-start(bf16[2,128,512]{1,2,0:T(8,128)(2,1)} %get-tuple-element.41), channel_id=1, source_target_pairs={{8,0},{10,2},{12,4},{14,6},{16,8},{18,10},{20,12},{22,14},{24,16},... | collective-permute-start | bytes 786440 | tf_op jit(solution)/shard_map/ppermute | solution.py:22
  110.3 20.3 %collective-permute-start.13 = (bf16[2,128,512]{1,2,0:T(8,128)(2,1)}, bf16[2,128,512]{1,2,0:T(8,128)(2,1)}, u32[]{:S(2)}, u32[]{:S(2)}) collective-permute-start(bf16[2,128,512]{1,2,0:T(8,128)(2,1)} %get-tuple-element.42), channel_id=1, source_target_pairs={{6,0},{8,2},{10,4},{12,6},{14,8},{16,10},{18,12},{20,14},{22,16},{... | collective-permute-start | bytes 786440 | tf_op jit(solution)/shard_map/ppermute | solution.py:22
  111.7 22.4 %collective-permute-start.12 = (bf16[2,128,512]{1,2,0:T(8,128)(2,1)}, bf16[2,128,512]{1,2,0:T(8,128)(2,1)}, u32[]{:S(2)}, u32[]{:S(2)}) collective-permute-start(bf16[2,128,512]{1,2,0:T(8,128)(2,1)} %get-tuple-element.43), channel_id=1, source_target_pairs={{4,0},{6,2},{8,4},{10,6},{12,8},{14,10},{16,12},{18,14},{20,16},{2... | collective-permute-start | bytes 786440 | tf_op jit(solution)/shard_map/ppermute | solution.py:22
  115.2 50.8 %collective-permute-start.10 = (bf16[128,640]{1,0:T(8,128)(2,1)}, bf16[128,640]{1,0:T(8,128)(2,1)}, u32[]{:S(2)}, u32[]{:S(2)}) collective-permute-start(bf16[128,640]{1,0:T(8,128)(2,1)} %slice.348), channel_id=1, source_target_pairs={{0,1},{1,0},{2,3},{3,2},{4,5},{5,4},{6,7},{7,6},{8,9},{9,8},{10,11... | collective-permute-start | bytes 491528 | tf_op jit(solution)/shard_map/ppermute | solution.py:74
  119.2 17.1 %copy-start.8 = (bf16[640,512]{1,0:T(8,128)(2,1)S(1)}, bf16[640,512]{1,0:T(8,128)(2,1)}, u32[]{:S(2)}) copy-start(bf16[640,512]{1,0:T(8,128)(2,1)} %copy.146) | copy-start | bytes 1966084
  135.7 9.2 %collective-permute-start.15 = (bf16[2,128,512]{1,2,0:T(8,128)(2,1)S(1)}, bf16[2,128,512]{1,2,0:T(8,128)(2,1)S(1)}, u32[]{:S(2)}, u32[]{:S(2)}) collective-permute-start(bf16[2,128,512]{1,2,0:T(8,128)(2,1)S(1)} %get-tuple-element.30), channel_id=1, source_target_pairs={{0,1},{1,0},{2,3},{3,2},{4,5},{5,4},{6,7},{7,6},{8,9},{9,8},{10,11... | collective-permute-start | bytes 786440 | tf_op jit(solution)/shard_map/ppermute | solution.py:74
  (57 other events, 183.6 us)
